TPU v7x, 128 devices: a whole 4x4x4 slice. The times are simulated.
128 devices in a mesh: gx: 4 (over x), yz: 32 (over z, y, core).
Axes of the slice: x: 4, y: 4, z: 4, core: 2. Of those that a mesh axis runs over, the one named last changes fastest.
Arguments:
- tokens: bfloat16 [4, 256, 18432], P('gx', None, 'yz'), may hold values from -6 to 6
- gain: float32 [18432], replicated, may hold values from 0.1 to 1.9
- w_query: bfloat16 [18432, 8192], P('gx', 'yz'), may hold values from -0.046875 to 0.046875
- w_keyval: bfloat16 [18432, 512], P('gx', 'yz'), may hold values from -0.09375 to 0.09375
- w_out: bfloat16 [8192, 18432], P('gx', 'yz'), may hold values from -0.375 to 0.375
- cache: bfloat16 [4, 2048, 512], P('gx', 'yz'), as said below
- lengths: int32 [4], P('gx'), may hold values from 1024 to 2048, as said below
Outputs:
- attended: bfloat16 [4, 256, 18432], P('gx', None, 'yz')
Inputs may be any that keep to these rules, and one draw needn't show every extreme that they name: `lengths`: some sequence has exactly 2048 filled slots and some exactly 1024. `cache`: cached keys are already rotated to their slot positions.
All inputs are finite; a program needn't handle non-finite values.
Results may differ from a plain program's by a relative error of at most 0.012.
The roundings to bfloat16 on the way count: a program that leaves them out, or rounds other values in their place, can miss the bound.
Values may be sent and summed in bfloat16 or wider, within the bound.
A program may use at most 128 MiB of HBM per device.

v0:
```python
import math

import jax
import jax.numpy as jnp
from jax import lax
from jax.sharding import PartitionSpec as P

HEAD = 256


def layer_norm(tokens, gain):
    values = tokens.astype(jnp.float32)
    mean = jnp.mean(values, axis=-1, keepdims=True)
    centered = values - mean
    spread = jnp.mean(centered * centered, axis=-1, keepdims=True)
    return (centered * lax.rsqrt(spread + 1e-06) * gain).astype(jnp.bfloat16)


def rotate(values, positions):
    width = values.shape[-1]
    half = width // 2
    freq = jnp.exp(jnp.arange(half, dtype=jnp.float32) * (-2.0 * math.log(10000.0) / width))
    angles = positions.astype(jnp.float32)[..., None] * freq
    cosine = jnp.cos(angles)[:, :, None, :]
    sine = jnp.sin(angles)[:, :, None, :]
    first = values[..., :half]
    second = values[..., half:]
    return jnp.concatenate(
        [first * cosine - second * sine, second * cosine + first * sine], axis=-1
    )


def absorb(carry, query, keys, values, mask, scale):
    largest, total, summed = carry
    scores = jnp.einsum("rchd,rpd->rhcp", query, keys, preferred_element_type=jnp.float32) * scale
    wide_mask = mask[:, None, :, :]
    block_top = jnp.max(jnp.where(wide_mask, scores, -1e30), axis=-1)
    new_top = jnp.maximum(largest, block_top)
    probs = jnp.exp(jnp.where(wide_mask, scores - new_top[..., None], -jnp.inf))
    factor = jnp.exp(largest - new_top)
    total = total * factor + jnp.sum(probs, axis=-1)
    summed = summed * factor[..., None] + jnp.einsum(
        "rhcp,rpd->rhcd", probs.astype(jnp.bfloat16), values, preferred_element_type=jnp.float32
    )
    return (new_top, total, summed)


def body(tokens, gain, w_query, w_keyval, w_out, cache, lengths):
    rows, span, _ = tokens.shape
    whole = lax.all_gather(tokens, "yz", axis=2, tiled=True)
    normed = layer_norm(whole, gain)
    flat = normed.reshape(rows * span, whole.shape[2])
    query_cols = w_query.shape[1]
    pair_cols = w_keyval.shape[1]
    left = flat
    query_raw = jnp.dot(
        left, lax.all_gather(w_query, "gx", axis=0, tiled=True), preferred_element_type=jnp.float32
    )
    pair_part = jnp.dot(
        left, lax.all_gather(w_keyval, "gx", axis=0, tiled=True), preferred_element_type=jnp.float32
    )
    heads_here = query_cols // HEAD
    steps = jnp.arange(span, dtype=jnp.int32)
    positions = lengths[:, None] + steps[None, :]
    query = rotate(query_raw.reshape(rows, span, heads_here, HEAD), positions).astype(jnp.bfloat16)
    keyval = lax.all_gather(
        pair_part.astype(jnp.bfloat16).reshape(rows, span, pair_cols), "yz", axis=2, tiled=True
    )
    fresh_keys = rotate(keyval[:, :, None, :HEAD].astype(jnp.float32), positions)[
        :, :, 0, :
    ].astype(jnp.bfloat16)
    fresh_values = keyval[:, :, HEAD:]
    scale = 1.0 / math.sqrt(HEAD)
    initial = (
        jnp.full((rows, heads_here, span), -1e30, jnp.float32),
        jnp.zeros((rows, heads_here, span), jnp.float32),
        jnp.zeros((rows, heads_here, span, HEAD), jnp.float32),
    )
    piece = lax.all_gather(cache, "yz", axis=1, tiled=True)
    count = piece.shape[1]
    slots = jnp.arange(count, dtype=jnp.int32)
    usable = slots[None, :] < lengths[:, None]
    mask = jnp.broadcast_to(usable[:, None, :], (rows, span, count))
    carry = absorb(initial, query, piece[:, :, :HEAD], piece[:, :, HEAD:], mask, scale)
    causal = (steps[:, None] >= steps[None, :])[None]
    largest, total, summed = absorb(carry, query, fresh_keys, fresh_values, causal, scale)
    heads_out = (summed / total[..., None]).astype(jnp.bfloat16)
    heads_out = heads_out.transpose(0, 2, 1, 3).reshape(rows * span, query_cols)
    all_heads = lax.all_gather(heads_out, "yz", axis=1, tiled=True)
    left = all_heads
    result = jnp.dot(
        left, lax.all_gather(w_out, "gx", axis=0, tiled=True), preferred_element_type=jnp.float32
    )
    return result.astype(jnp.bfloat16).reshape(rows, span, w_out.shape[1])


def solution(mesh):
    return jax.shard_map(
        body,
        mesh=mesh,
        in_specs=(
            P("gx", None, "yz"),
            P(),
            P("gx", "yz"),
            P("gx", "yz"),
            P("gx", "yz"),
            P("gx", "yz", None),
            P("gx"),
        ),
        out_specs=P("gx", None, "yz"),
        check_vma=False,
    )
```

profile of v0, /device:TPU:1, one launch (start us, length us, event | category | flops | bytes accessed | tf_op | source)
XLA Modules:
  0.0 369.3 jit_solution(7550760167740069210)
XLA Ops:
  6.5 0.0 all-gather.7.cloned.1.call-start
  6.5 0.7 all-gather.7.cloned.1.call-update
  7.3 0.0 all-gather.9.cloned.1.call-start
  7.3 0.7 all-gather.9.cloned.1.call-update
  8.0 0.0 all-gather.11.cloned.1.call-start
  8.1 0.7 all-gather.11.cloned.1.call-update
  8.7 0.0 all-gather.15.cloned.1.call-start
  8.8 0.5 all-gather.15.cloned.1.call-update
  9.3 0.0 all-gather.13.cloned.1.call-start
  10.0 12.7 %all_gather.24 = bf16[18432,16]{0,1:T(8,128)(2,1)S(1)} all-gather(bf16[4608,16]{0,1:T(8,128)(2,1)} %param.10), channel_id=1, replica_groups=mesh['gx'=4,'yz'=32] {'gx'}, dimensions={0}, use_global_device_ids=true | all-gather | bytes 737280 | tf_op jit(solution)/shard_map/all_gather | solution.py:60
  22.7 46.1 %all-gather.7.cloned.1.call-done = bf16[1,256,18432]{1,2,0:T(8,128)(2,1)} async-done(((bf16[1,256,576]{1,2,0:T(8,128)(2,1)}), bf16[1,256,18432]{1,2,0:T(8,128)(2,1)}) %all-gather.7.cloned.1.call-update) | async-done | bytes 9437200 | tf_op jit(solution)/shard_map/all_gather | solution.py:50
  68.8 0.0 copy-start
  68.8 0.0 copy-start.1
  68.8 7.0 %convert_reduce_fusion = f32[256]{0:T(256)S(1)} fusion(bf16[1,256,18432]{1,2,0:T(8,128)(2,1)} %all-gather.7.cloned.1.call-done), kind=kLoop, calls=%fused_computation.1 | loop fusion | flops 9436928 | bytes 9438208 | tf_op jit(solution)/shard_map/reduce_sum | solution.py:13
  75.8 0.0 copy-done
  75.8 2.7 fusion.2
  78.5 0.0 copy-done.1
  78.5 3.0 fusion.21
  81.5 24.7 %all-gather = bf16[256,512]{0,1:T(8,128)(2,1)S(1)} all-gather(bf16[256,16]{0,1:T(8,128)(2,1)S(1)} %fusion.21), channel_id=2, replica_groups=mesh['gx'=4,'yz'=32] {'yz'}, dimensions={1}, use_global_device_ids=true | all-gather | bytes 270336 | tf_op jit(solution)/shard_map/all_gather | solution.py:66
  106.3 55.3 %all-gather.9.cloned.1.call-done = bf16[18432,256]{1,0:T(8,128)(2,1)} async-done(((bf16[4608,256]{1,0:T(8,128)(2,1)}), bf16[18432,256]{1,0:T(8,128)(2,1)}) %all-gather.9.cloned.1.call-update) | async-done | bytes 9437200 | tf_op jit(solution)/shard_map/all_gather | solution.py:57
  161.5 11.4 %fusion.16 = f32[1,256,1,256]{1,3,2,0:T(8,128)S(1)} fusion(bf16[18432,256]{1,0:T(8,128)(2,1)} %all-gather.9.cloned.1.call-done, bf16[1,256,18432]{1,2,0:T(8,128)(2,1)} %all-gather.7.cloned.1.call-done, f32[18432]{0:T(1024)S(1)} %copy-done.1, f32[256]{0:T(256)S(1)} %add_rsqrt_fusion, f32[256]{0:T(256)S(1)} %broadcast_multiply_fusion), kind=kOutput, calls=%fused_computation.22 | convolution fusion | flops 2439512064 | bytes 19212288 | tf_op jit(solution)/shard_map/dot_general | solution.py:56
  173.0 0.6 fusion.44
  173.6 0.2 select_reduce_fusion.1
  173.8 35.4 %all-gather.11.cloned.1.call-done = bf16[1,2048,512]{2,1,0:T(8,128)(2,1)} async-done(((bf16[1,64,512]{2,1,0:T(8,128)(2,1)}), bf16[1,2048,512]{2,1,0:T(8,128)(2,1)}) %all-gather.11.cloned.1.call-update) | async-done | bytes 2097168 | tf_op jit(solution)/shard_map/all_gather | solution.py:79
  209.2 1.8 select_reduce_fusion
  211.1 0.1 fusion.29
  211.1 0.5 fusion.7
  211.6 1.8 fusion.19
  213.4 0.9 fusion.20
  214.3 0.0 all-gather.13.cloned.1.call-update
  214.3 87.2 %all-gather.15.cloned.1.call-done = bf16[8192,576]{0,1:T(8,128)(2,1)} async-done(((bf16[2048,576]{0,1:T(8,128)(2,1)}), bf16[8192,576]{0,1:T(8,128)(2,1)}) %all-gather.15.cloned.1.call-update) | async-done | bytes 9437200 | tf_op jit(solution)/shard_map/all_gather | solution.py:92
  301.5 52.9 %all-gather.13.cloned.1.call-done = bf16[256,8192]{1,0:T(8,128)(2,1)} async-done(((bf16[256,256]{1,0:T(8,128)(2,1)}), bf16[256,8192]{1,0:T(8,128)(2,1)}) %all-gather.13.cloned.1.call-update) | async-done | bytes 4194320 | tf_op jit(solution)/shard_map/all_gather | solution.py:89
  354.4 8.3 %fusion.13 = bf16[1,256,576]{1,2,0:T(8,128)(2,1)} fusion(bf16[256,8192]{1,0:T(8,128)(2,1)} %all-gather.13.cloned.1.call-done, bf16[8192,576]{0,1:T(8,128)(2,1)} %all-gather.15.cloned.1.call-done), kind=kOutput, calls=%fused_computation.17 | convolution fusion | flops 2416066560 | bytes 13926400 | tf_op jit(solution)/shard_map/dot_general | solution.py:91
  (8 shorter events, 0.1 us)
Async XLA Ops:
  6.5 62.3 %all-gather.7.cloned.1.call-start = ((), (), s32[]{:S(2)}) async-start(), calls=%async_computation | async-start | bytes 9732096 | tf_op jit(solution)/shard_map/all_gather | solution.py:50
  7.3 154.3 %all-gather.9.cloned.1.call-start = ((), (), s32[]{:S(2)}) async-start(), calls=%async_computation.1 | async-start | bytes 11796480 | tf_op jit(solution)/shard_map/all_gather | solution.py:57
  8.0 201.2 %all-gather.11.cloned.1.call-start = ((), (), s32[]{:S(2)}) async-start(), calls=%async_computation.2 | async-start | bytes 2162688 | tf_op jit(solution)/shard_map/all_gather | solution.py:79
  8.7 292.8 %all-gather.15.cloned.1.call-start = ((), (), s32[]{:S(2)}) async-start(), calls=%async_computation.4 | async-start | bytes 11796480 | tf_op jit(solution)/shard_map/all_gather | solution.py:92
  9.3 345.1 %all-gather.13.cloned.1.call-start = ((), (), s32[]{:S(2)}) async-start(), calls=%async_computation.3 | async-start | bytes 4325376 | tf_op jit(solution)/shard_map/all_gather | solution.py:89
  68.8 7.0 %copy-start = (bf16[1,256,18432]{1,2,0:T(8,128)(2,1)S(1)}, bf16[1,256,18432]{1,2,0:T(8,128)(2,1)}, u32[]{:S(2)}) copy-start(bf16[1,256,18432]{1,2,0:T(8,128)(2,1)} %all-gather.7.cloned.1.call-done) | copy-start | bytes 28311556
  68.8 9.7 %copy-start.1 = (f32[18432]{0:T(1024)S(1)}, f32[18432]{0:T(1024)}, u32[]{:S(2)}) copy-start(f32[18432]{0:T(1024)} %param.8) | copy-start | bytes 221188
Sparse Core Ops, SparseCore 0:
  9.6 59.1 all-gather.6
  70.5 91.0 all-gather.8
  163.8 45.3 all-gather.10
  210.8 90.7 all-gather.14
  303.6 50.8 all-gather.12
where the time goes:
time: 369 us
  waiting for transfers between devices  279 us (76%)
  blocking collectives  37.4 us (10%)
  matrix products  27.5 us (7%)
  between operations  13.9 us (4%)
  other arithmetic  10.9 us (3%)
    all_gather x1, waiting for transfers between devices, body(): lax.all_gather(w_out, 'gx', axis=0, tiled=True)  87.2 us
    all_gather x1, waiting for transfers between devices, body(): lax.all_gather(w_query, 'gx', axis=0, tiled=True)  55.3 us
    all_gather x1, waiting for transfers between devices, body(): all_heads = lax.all_gather(heads_out, 'yz', axis=1, tiled=True)  52.9 us
    all_gather x1, waiting for transfers between devices, body(): whole = lax.all_gather(tokens, 'yz', axis=2, tiled=True)  46.1 us
    all_gather x1, waiting for transfers between devices, body(): piece = lax.all_gather(cache, 'yz', axis=1, tiled=True)  35.4 us
    all_gather x1, blocking collectives, body(): lax.all_gather(pair_part.astype(jnp.bfloat16).reshape(rows, span, pair_co...  24.7 us
    all_gather x1, blocking collectives, body(): lax.all_gather(w_keyval, 'gx', axis=0, tiled=True)  12.7 us
    dot_general x1, matrix products, body(): jnp.dot(left, lax.all_gather(w_query, 'gx', axis=0, tiled=True), preferre...  11.4 us
  transfers between devices with their start and end apart: 5, of which 5 were waited for; matrix products, arithmetic and copies ran while one was open for 8% of the time, Pallas kernels for 0%

commit v1 on v0

v1 whole, which is shorter than its diff:
```python
import functools
import math

import jax
import jax.numpy as jnp
from jax import lax
from jax.experimental import pallas as pl
from jax.experimental.pallas import tpu as pltpu
from jax.sharding import PartitionSpec as P

MESH = pl.DeviceIdType.MESH
HEAD = 256
F32 = jnp.float32
BF16 = jnp.bfloat16


class Wires:
    def __init__(self, send, recv):
        self.send, self.recv, self.used, self.all = send, recv, 0, []

    def __call__(self, src, dst, target):
        k = self.used
        self.used += 1
        copy = pltpu.make_async_remote_copy(
            src_ref=src, dst_ref=dst, send_sem=self.send.at[k], recv_sem=self.recv.at[k],
            device_id=target, device_id_type=MESH,
        )
        copy.start()
        self.all.append(copy)
        return copy


def gather_plane(wires, unit, here, peer_y, peer_z, y, z, on_a, on_b):
    near = lambda v, d: lax.rem(v + d + 4, 4)
    yj = [y, near(y, -1), near(y, 1), near(y, 2)]
    zj = [z, near(z, -1), near(z, 1), near(z, 2)]

    def a(zz, yy, first=0, count=2):
        return unit(zz, yy, first, count)

    def b(zz, yy, first=2, count=2):
        return unit(zz, yy, first, count)

    def send(ref, target):
        return wires(ref, ref, target)

    zp, zm, yp, ym = [None] * 4, [None] * 4, [None] * 4, [None] * 4
    zfp, zfm, yfp, yfm = [None] * 4, [None] * 4, [None] * 4, [None] * 4

    def spread_a(j):
        zp[j] = send(a(z, yj[j]), peer_z(1))
        zm[j] = send(a(z, yj[j]), peer_z(-1))

    def spread_b(j):
        yp[j] = send(b(zj[j], y), peer_y(1))
        ym[j] = send(b(zj[j], y), peer_y(-1))

    def pass_a(j):
        zp[j].wait_recv()
        zfp[j] = send(a(zj[1], yj[j], 0, 1), peer_z(1))
        zm[j].wait_recv()
        zfm[j] = send(a(zj[2], yj[j], 1, 1), peer_z(-1))

    def pass_b(j):
        yp[j].wait_recv()
        yfp[j] = send(b(zj[j], yj[1], 2, 1), peer_y(1))
        ym[j].wait_recv()
        yfm[j] = send(b(zj[j], yj[2], 3, 1), peer_y(-1))

    a1p = send(a(z, y), peer_y(1))
    b1p = send(b(z, y), peer_z(1))
    a1m = send(a(z, y), peer_y(-1))
    b1m = send(b(z, y), peer_z(-1))
    spread_a(0)
    spread_b(0)
    a1p.wait_recv()
    a2p = send(a(z, yj[1], 0, 1), peer_y(1))
    spread_a(1)
    b1p.wait_recv()
    b2p = send(b(zj[1], y, 2, 1), peer_z(1))
    spread_b(1)
    a1m.wait_recv()
    a2m = send(a(z, yj[2], 1, 1), peer_y(-1))
    spread_a(2)
    b1m.wait_recv()
    b2m = send(b(zj[2], y, 3, 1), peer_z(-1))
    spread_b(2)
    pass_a(0)
    pass_b(0)
    a2p.wait_recv()
    a2m.wait_recv()
    spread_a(3)
    b2p.wait_recv()
    b2m.wait_recv()
    spread_b(3)
    for j in range(1, 4):
        pass_a(j)
        pass_b(j)
        zfp[j - 1].wait_recv()
        zfm[j - 1].wait_recv()
        yfp[j - 1].wait_recv()
        yfm[j - 1].wait_recv()
    for last in (zfp[3], zfm[3], yfp[3], yfm[3]):
        last.wait_recv()


def kernel(
    tokens, gain, w_query, w_keyval, w_out, cache, lengths, cos, sin, cos_t, sin_t, out,
    raw, stats, normed, whole, wq, kv_pair, wo, partial, q_send, kv_part, kv_send, q_recv, kv_recv,
    kv_t, slots, scores, weights, queries, totals, heads, heads_z, heads_all, o_send, o_recv,
    send_sem, recv_sem, local_sem,
):
    x = lax.axis_index("gx")
    yz = lax.axis_index("yz")
    z, y, c = yz // 8, (yz // 2) % 4, yz % 2
    near = lambda v, d: lax.rem(v + d + 4, 4)

    def device(xx, zz, yy, cc):
        return (xx, zz * 8 + yy * 2 + cc)

    peer_x = lambda d, dc=0: device(near(x, d), z, y, lax.rem(c + dc, 2))
    peer_y = lambda d: device(x, z, near(y, d), c)
    peer_z = lambda d, dc=0: device(x, near(z, d), y, lax.rem(c + dc, 2))
    sibling = device(x, z, y, 1 - c)

    barrier = pltpu.get_barrier_semaphore()
    peers = [sibling]
    for d in (1, 2, 3):
        peers += [peer_x(d), peer_x(d, 1), peer_z(d), peer_z(d, 1), peer_y(d)]
    for p in peers:
        pl.semaphore_signal(barrier, inc=1, device_id=p, device_id_type=MESH)

    locals_ = []

    def local(src, dst):
        copy = pltpu.make_async_copy(src, dst, local_sem.at[len(locals_)])
        copy.start()
        locals_.append(copy)
        return copy

    own_raw = local(tokens.at[0, pl.ds(pl.multiple_of(c * 128 + z * 32, 32), 32), :], raw.at[z, c])
    own_wq = local(w_query, wq.at[:, pl.ds(pl.multiple_of(c * 256, 256), 256)])
    own_kv = local(w_keyval, kv_pair.at[c])
    own_wo = local(w_out, wo.at[c])
    own_slots = local(cache.at[0], slots.at[pl.ds(pl.multiple_of(yz * 64, 64), 64), :])

    pl.semaphore_wait(barrier, len(peers))
    wires = Wires(send_sem, recv_sem)

    first = []
    for d in (0, 1, 2, 3):
        for dc in (0, 1):
            if d or dc:
                zz, cc = near(z, d), lax.rem(c + dc, 2)
                rows = pl.ds(pl.multiple_of(cc * 128 + zz * 32, 32), 32)
                first.append(wires(tokens.at[0, rows, :], raw.at[z, c], device(x, zz, y, cc)))
    slot_rows = lambda zz, yy: slots.at[pl.ds(pl.multiple_of((zz * 8 + yy * 2 + c) * 64, 64), 64), :]
    own_slots.wait()
    cache_y = [wires(slot_rows(z, y), slot_rows(z, y), peer_y(d)) for d in (1, 2, 3)]
    wq_copy = wires(w_query, wq.at[:, pl.ds(pl.multiple_of(c * 256, 256), 256)], sibling)
    kv_copy = wires(w_keyval, kv_pair.at[c], sibling)
    wo_copy = wires(w_out, wo.at[c], sibling)

    own_raw.wait()
    for copy in first:
        copy.wait_recv()
    values = raw[...].astype(F32)
    mean = jnp.sum(jnp.sum(values, axis=(0, 1)), axis=-1, keepdims=True) * (1.0 / 4608)
    centered = values - mean[None, None]
    square = jnp.sum(jnp.sum(centered * centered, axis=(0, 1)), axis=-1, keepdims=True)
    lane = lax.broadcasted_iota(jnp.int32, (32, 128), 1)
    stats[y] = jnp.where(lane < 64, mean, square)
    stat_copies = [wires(stats.at[y], stats.at[y], peer_y(d)) for d in (1, 2, 3)]
    for copy in stat_copies:
        copy.wait_recv()
    means = [stats[k][:, 0:1] for k in range(4)]
    squares = [stats[k][:, 64:65] for k in range(4)]
    mean = (means[0] + means[1] + means[2] + means[3]) * 0.25
    spread = squares[0] + squares[1] + squares[2] + squares[3]
    for k in range(4):
        spread = spread + 4608.0 * (means[k] - mean) * (means[k] - mean)
    scale = lax.rsqrt(spread * (1.0 / 18432) + 1e-6)
    for i in range(4):
        both = []
        for k in range(2):
            g = gain[pl.ds(i * 8 + y * 2 + k, 1), :]
            both.append((raw[i, k].astype(F32) - mean) * scale * g)
        normed[i] = jnp.concatenate(both, axis=-1).astype(BF16)

    def unit(zz, yy, start, count):
        return whole.at[
            pl.ds(pl.multiple_of(zz * 128 + start * 32, 32), count * 32),
            pl.ds(pl.multiple_of(yy * 1152, 128), 1152),
        ]

    mine = local(normed.at[x], unit(z, y, x, 1))
    second = [wires(normed.at[near(x, d)], unit(z, y, x, 1), peer_x(d)) for d in (1, 3, 2)]
    for copy in cache_y:
        copy.wait_recv()
    cache_z = []
    for k in range(4):
        cache_z.append(wires(slot_rows(z, k), slot_rows(z, k), sibling))
    for d in (1, 3, 2):
        for k in range(4):
            for dc in (0, 1):
                cache_z.append(wires(slot_rows(z, k), slot_rows(z, k), peer_z(d, dc)))
    mine.wait()
    for copy in second:
        copy.wait_recv()
    gather_plane(wires, unit, None, peer_y, peer_z, y, z, None, None)

    for copy in (own_wq, own_kv, own_wo):
        copy.wait()
    for copy in (wq_copy, kv_copy):
        copy.wait_recv()

    @pl.loop(0, 18)
    def _(s):
        rows = pl.ds(pl.multiple_of(s * 256, 256), 256)
        pair = jnp.concatenate(
            [kv_pair[0, rows, :].astype(F32), kv_pair[1, rows, :].astype(F32), jnp.zeros((256, 96), F32)], axis=-1
        )
        wq[rows, 512:640] = pair.astype(BF16)

    @pl.loop(0, 4)
    def _(r):
        rows = pl.ds(pl.multiple_of(r * 128, 128), 128)
        acc = jnp.dot(whole[rows, :], wq[...], preferred_element_type=F32)
        partial[r] = acc[:, :512]
        q_send[r] = acc[:, :512].astype(BF16)
        kv_part[r] = acc[:, 512:]

    for b in range(4):
        block = jnp.concatenate([kv_part[r, b * 32:(b + 1) * 32, :] for r in range(4)], axis=0)
        kv_send[b] = block.T[:32, :]
    thirds = []
    for d in (1, 3, 2):
        xx = near(x, d)
        thirds.append(wires(kv_send.at[xx], kv_recv.at[x], peer_x(d)))
    for d in (1, 3, 2):
        rows = pl.ds(pl.multiple_of(near(x, d) * 32, 32), 32)
        thirds.append(wires(q_send.at[:, rows, :], q_recv.at[x], peer_x(d)))
    for copy in thirds[:3]:
        copy.wait_recv()
    total = kv_send[x]
    for d in (1, 2, 3):
        total = total + kv_recv[near(x, d)]
    kv_block = lambda zz, yy: kv_t.at[
        pl.ds(pl.multiple_of((zz * 4 + yy) * 32, 32), 32), pl.ds(pl.multiple_of(c * 128, 128), 128)
    ]
    kv_t[pl.ds(pl.multiple_of((z * 4 + y) * 32, 32), 32), pl.ds(pl.multiple_of(c * 128, 128), 128)] = total.astype(BF16)
    kv_y = [wires(kv_block(z, y), kv_block(z, y), peer_y(d)) for d in (1, 2, 3)]
    for copy in kv_y:
        copy.wait_recv()
    kv_rows = kv_t.at[pl.ds(pl.multiple_of(z * 128, 128), 128), pl.ds(pl.multiple_of(c * 128, 128), 128)]
    kv_z = [wires(kv_rows, kv_rows, sibling)]
    for d in (1, 3, 2):
        for dc in (0, 1):
            kv_z.append(wires(kv_rows, kv_rows, peer_z(d, dc)))

    for copy in thirds[3:]:
        copy.wait_recv()
    mine_rows = pl.ds(pl.multiple_of(x * 32, 32), 32)
    query = partial[:, mine_rows, :].reshape(128, 512)
    for d in (1, 2, 3):
        query = query + q_recv[near(x, d)].reshape(128, 512).astype(F32)
    half_rows = pl.ds(pl.multiple_of(c * 128, 128), 128)
    cosine, sine = cos[half_rows, :], sin[half_rows, :]
    for h in range(2):
        u, w = query[:, h * 256:h * 256 + 128], query[:, h * 256 + 128:h * 256 + 256]
        queries[h * 128:(h + 1) * 128, 0:128] = (u * cosine - w * sine).astype(BF16)
        queries[h * 128:(h + 1) * 128, 128:256] = (w * cosine + u * sine).astype(BF16)
    for copy in cache_z:
        copy.wait_recv()
    inv = 1.0 / math.sqrt(HEAD)
    contract = (((1,), (1,)), ((), ()))

    @pl.loop(0, 8)
    def _(k):
        at = pl.ds(pl.multiple_of(k * 256, 256), 256)
        s = lax.dot_general(queries[...], slots[at, 0:256], contract, preferred_element_type=F32) * inv
        col = k * 256 + lax.broadcasted_iota(jnp.int32, (256, 256), 1)
        scores[:, at] = jnp.where(col < lengths[0], s, -1e30)

    for copy in kv_z:
        copy.wait_recv()
    u, w = kv_t[0:128, :].astype(F32), kv_t[128:256, :].astype(F32)
    ct, st = cos_t[...], sin_t[...]
    fresh = jnp.concatenate([u * ct - w * st, w * ct + u * st], axis=0).astype(BF16)
    s = jnp.dot(queries[...], fresh, preferred_element_type=F32) * inv
    t = c * 128 + lax.rem(lax.broadcasted_iota(jnp.int32, (256, 256), 0), 128)
    t2 = lax.broadcasted_iota(jnp.int32, (256, 256), 1)
    scores[:, 2048:2304] = jnp.where(t2 <= t, s, -1e30)

    @pl.loop(0, 8)
    def _(k):
        at = pl.ds(pl.multiple_of(k * 32, 32), 32)
        s = scores[at, :]
        p = jnp.exp(s - jnp.max(s, axis=-1, keepdims=True))
        totals[at, :] = jnp.broadcast_to(jnp.sum(p, axis=-1, keepdims=True), (32, 128))
        weights[at, :] = p.astype(BF16)

    for h in range(2):
        at = slice(h * 128, (h + 1) * 128)
        summed = jnp.dot(weights[at, 0:2048], slots[:, 256:512], preferred_element_type=F32)
        summed += lax.dot_general(weights[at, 2048:2304], kv_t[256:512, :], contract, preferred_element_type=F32)
        heads[:, h * 256:(h + 1) * 256] = (summed / totals[at, 0:1]).astype(BF16)

    fourth = []
    for d in (1, 3, 2):
        rows = pl.ds(pl.multiple_of(near(z, d) * 32, 32), 32)
        fourth.append(wires(heads.at[rows, :], heads_z.at[z], peer_z(d)))
    own = local(heads.at[pl.ds(pl.multiple_of(z * 32, 32), 32), :], heads_z.at[z])

    def head_unit(zz, yy, start, count):
        return heads_all.at[
            pl.ds(pl.multiple_of(zz * 128 + start * 32, 32), count * 32),
            pl.ds(pl.multiple_of(yy * 512, 128), 512),
        ]

    own.wait()
    for copy in fourth:
        copy.wait_recv()
    mine = local(heads_z.at[x], head_unit(z, y, x, 1))
    fifth = [wires(heads_z.at[near(x, d)], head_unit(z, y, x, 1), peer_x(d)) for d in (1, 3, 2)]
    mine.wait()
    for copy in fifth:
        copy.wait_recv()
    gather_plane(wires, head_unit, None, peer_y, peer_z, y, z, None, None)

    wo_copy.wait_recv()
    last = []
    for r in range(4):
        for k in range(2):
            o_send[k, r] = jnp.dot(
                heads_all[r * 128:(r + 1) * 128, :], wo[k], preferred_element_type=F32
            ).astype(BF16)
    for d in (1, 3, 2, 0):
        rows = pl.ds(pl.multiple_of(near(x, d) * 32, 32), 32)
        for dc in (0, 1):
            if d or dc:
                cc = lax.rem(c + dc, 2)
                last.append(wires(o_send.at[cc, :, rows, :], o_recv.at[x, c], peer_x(d, dc)))
    own = local(o_send.at[c, :, pl.ds(pl.multiple_of(x * 32, 32), 32), :], o_recv.at[x, c])
    own.wait()
    for copy in last:
        copy.wait_recv()
    for k in range(2):
        total = o_recv[0, k].astype(F32)
        for xx in (1, 2, 3):
            total = total + o_recv[xx, k].astype(F32)
        out[0, k * 128:(k + 1) * 128, :] = total.reshape(128, 576).astype(BF16)

    for copy in wires.all:
        copy.wait_send()


def tables(lengths):
    half = HEAD // 2
    freq = jnp.exp(jnp.arange(half, dtype=F32) * (-2.0 * math.log(10000.0) / HEAD))
    positions = (lengths[0] + jnp.arange(256, dtype=jnp.int32)).astype(F32)
    angles = positions[:, None] * freq[None, :]
    angles_t = freq[:, None] * positions[None, :]
    return jnp.cos(angles), jnp.sin(angles), jnp.cos(angles_t), jnp.sin(angles_t)


def body(tokens, gain, w_query, w_keyval, w_out, cache, lengths):
    hbm = pl.BlockSpec(memory_space=pl.ANY)
    vmem = pl.BlockSpec(memory_space=pltpu.VMEM)
    smem = pl.BlockSpec(memory_space=pltpu.SMEM)
    return pl.pallas_call(
        kernel,
        out_shape=jax.ShapeDtypeStruct((1, 256, 576), BF16),
        in_specs=[hbm, vmem, hbm, hbm, hbm, hbm, smem, vmem, vmem, vmem, vmem],
        out_specs=vmem,
        scratch_shapes=[
            pltpu.VMEM((4, 2, 32, 576), BF16),
            pltpu.VMEM((4, 32, 128), F32),
            pltpu.VMEM((4, 32, 1152), BF16),
            pltpu.VMEM((512, 4608), BF16),
            pltpu.VMEM((4608, 640), BF16),
            pltpu.VMEM((2, 4608, 16), BF16),
            pltpu.VMEM((2, 2048, 576), BF16),
            pltpu.VMEM((4, 128, 512), F32),
            pltpu.VMEM((4, 128, 512), BF16),
            pltpu.VMEM((4, 128, 128), F32),
            pltpu.VMEM((4, 32, 128), F32),
            pltpu.VMEM((4, 4, 32, 512), BF16),
            pltpu.VMEM((4, 32, 128), F32),
            pltpu.VMEM((512, 256), BF16),
            pltpu.VMEM((2048, 512), BF16),
            pltpu.VMEM((256, 2304), F32),
            pltpu.VMEM((256, 2304), BF16),
            pltpu.VMEM((256, 256), BF16),
            pltpu.VMEM((256, 128), F32),
            pltpu.VMEM((128, 512), BF16),
            pltpu.VMEM((4, 32, 512), BF16),
            pltpu.VMEM((512, 2048), BF16),
            pltpu.VMEM((2, 4, 128, 576), BF16),
            pltpu.VMEM((4, 2, 4, 32, 576), BF16),
            pltpu.SemaphoreType.DMA((176,)),
            pltpu.SemaphoreType.DMA((176,)),
            pltpu.SemaphoreType.DMA((16,)),
        ],
        compiler_params=pltpu.CompilerParams(
            collective_id=0, has_side_effects=True, vmem_limit_bytes=56 * 1024 * 1024
        ),
    )(
        tokens, gain.reshape(32, 576), w_query, w_keyval, w_out, cache, lengths, *tables(lengths)
    )


def solution(mesh):
    return jax.shard_map(
        body,
        mesh=mesh,
        in_specs=(
            P("gx", None, "yz"),
            P(),
            P("gx", "yz"),
            P("gx", "yz"),
            P("gx", "yz"),
            P("gx", "yz", None),
            P("gx"),
        ),
        out_specs=P("gx", None, "yz"),
        check_vma=False,
    )
```

time: 369 us -> 148 us (0.40)
  waiting for transfers between devices: 279 us -> 0 us
  Pallas kernels: 0 us -> 134 us
  blocking collectives: 37.4 us -> 0 us
  matrix products: 27.5 us -> 0 us
  between operations: 13.9 us -> 0.83 us
  local copies, waits for them, and re-layouts: 0.01 us -> 10.2 us
  other arithmetic: 10.9 us -> 2.51 us
    all_gather x5 -> x0, waiting for transfers between devices: 277 us -> none  [the longest x1 87.2 us: body(): lax.all_gather(w_out, 'gx', axis=0, tiled=True)]
    pallas_call x0 -> x1, Pallas kernels: none -> 134 us  [body(): pl.pallas_call(kernel, out_shape=jax.ShapeDtypeStruct((1, 256, 576), BF16...]
    all_gather x2 -> x0, blocking collectives: 37.4 us -> none  [the longest x1 24.7 us: body(): lax.all_gather(pair_part.astype(jnp.bfloat16).reshape(rows, span, pair_co...]
    dot_general x7 -> x0, matrix products: 27.5 us -> none  [the longest x1 11.4 us: body(): jnp.dot(left, lax.all_gather(w_query, 'gx', axis=0, tiled=True), preferre...]
    reduce_sum x4 -> x0, other arithmetic: 10.3 us -> none  [the longest x1 7.01 us: layer_norm(): mean = jnp.mean(values, axis=-1, keepdims=True)]
    unnamed x4 -> x5, local copies, waits for them, and re-layouts: 0.01 us -> 6.78 us
  transfers between devices with their start and end apart: 5 -> 0, of which waited for: 5 -> 0; matrix products, arithmetic and copies ran while one was open for 8% -> 0% of each run, Pallas kernels for 0% -> 0%
where the time goes in v1:
time: 148 us
  Pallas kernels  134 us (91%)
  local copies, waits for them, and re-layouts  10.2 us (7%)
  other arithmetic  2.51 us (2%)
    pallas_call x1, Pallas kernels, body(): pl.pallas_call(kernel, out_shape=jax.ShapeDtypeStruct((1, 256, 576), BF16...  134 us
    unnamed x5, local copies, waits for them, and re-layouts  6.78 us

profile of v1, /device:TPU:1, one launch (start us, length us, event | category | flops | bytes accessed | tf_op | source)
XLA Modules:
  0.0 147.9 jit_solution(9318899497064218830)
XLA Ops:
  0.0 0.0 copy-start
  0.8 1.6 %reshape.23.gain = f32[32,576]{1,0:T(8,128)} reshape(f32[18432]{0:T(1024)} %param.8) | data formatting | bytes 147456 | tf_op jit(solution)/shard_map/reshape | solution.py:409
  2.4 1.2 multiply_sine_fusion.1
  3.7 1.3 multiply_sine_fusion
  4.9 1.9 %copy.8.tokens = bf16[1,256,576]{2,1,0:T(8,128)(2,1)} copy(bf16[1,256,576]{1,2,0:T(8,128)(2,1)} %param.7) | data formatting | bytes 589824 | tf_op args[0]
  6.8 2.3 %copy.9.w_keyval = bf16[4608,16]{1,0:T(8,128)(2,1)} copy(bf16[4608,16]{0,1:T(8,128)(2,1)} %param.10) | data formatting | bytes 294912 | tf_op args[3]
  9.1 0.0 copy-done
  9.1 2.6 %copy.10.w_out = bf16[2048,576]{1,0:T(8,128)(2,1)} copy(bf16[2048,576]{0,1:T(8,128)(2,1)S(1)} %copy-done) | data formatting | bytes 4718592 | tf_op args[4]
  11.7 134.4 %shard_map.73 = bf16[1,256,576]{2,1,0:T(8,128)(2,1)} custom-call(bf16[1,256,576]{2,1,0:T(8,128)(2,1)} %copy.8.tokens, f32[32,576]{1,0:T(8,128)} %reshape.23.gain, bf16[4608,256]{1,0:T(8,128)(2,1)} %w_query.1, bf16[4608,16]{1,0:T(8,128)(2,1)} %copy.9.w_keyval, bf16[2048,576]{1,0:T(8,128)(2,1)} %copy.10.w_out, bf16[1,64,512]{2,1,0:T(8,128)(2,1)} %cache.1, ...), custom_call_target="tpu_custom_call" | custom-call | tf_op jit(solution)/shard_map/pallas_call | solution.py:371
  146.1 1.8 %copy.11 = bf16[1,256,576]{1,2,0:T(8,128)(2,1)} copy(bf16[1,256,576]{2,1,0:T(8,128)(2,1)} %shard_map.73) | data formatting | bytes 589824 | tf_op jit(solution)/shard_map/pallas_call | solution.py:371
  (2 shorter events, 0.0 us)
Async XLA Ops:
  0.0 9.1 %copy-start = (bf16[2048,576]{0,1:T(8,128)(2,1)S(1)}, bf16[2048,576]{0,1:T(8,128)(2,1)}, u32[]{:S(2)}) copy-start(bf16[2048,576]{0,1:T(8,128)(2,1)} %param.11) | copy-start | bytes 7077892

commit v2 on v0

v2 whole, which is shorter than its diff:
```python
import math

import jax
import jax.numpy as jnp
from jax import lax
from jax.experimental import pallas as pl
from jax.experimental.pallas import tpu as pltpu
from jax.sharding import PartitionSpec as P

MESH = pl.DeviceIdType.MESH
HEAD = 256
F32 = jnp.float32
BF16 = jnp.bfloat16
LEFT = (((0,), (0,)), ((), ()))


class Wires:
    def __init__(self, send, recv):
        self.send, self.recv, self.used, self.all = send, recv, 0, []

    def __call__(self, src, dst, target):
        k = self.used
        self.used += 1
        copy = pltpu.make_async_remote_copy(
            src_ref=src, dst_ref=dst, send_sem=self.send.at[k], recv_sem=self.recv.at[k],
            device_id=target, device_id_type=MESH,
        )
        copy.start()
        self.all.append(copy)
        return copy


def near(v, d):
    return lax.rem(v + d + 4, 4)


def gather_plane(wires, unit, peer_y, peer_z, y, z, on_a=lambda j: None):
    yj = [y, near(y, -1), near(y, 1), near(y, 2)]
    zj = [z, near(z, -1), near(z, 1), near(z, 2)]

    def send(ref, target):
        return wires(ref, ref, target)

    zp, zm, yp, ym = [None] * 4, [None] * 4, [None] * 4, [None] * 4
    zfp, zfm, yfp, yfm = [None] * 4, [None] * 4, [None] * 4, [None] * 4

    def spread_a(j):
        zp[j] = send(unit(z, yj[j], 0, 2), peer_z(1))
        zm[j] = send(unit(z, yj[j], 0, 2), peer_z(-1))

    def spread_b(j):
        yp[j] = send(unit(zj[j], y, 2, 2), peer_y(1))
        ym[j] = send(unit(zj[j], y, 2, 2), peer_y(-1))

    def pass_a(j):
        zp[j].wait_recv()
        zfp[j] = send(unit(zj[1], yj[j], 0, 1), peer_z(1))
        zm[j].wait_recv()
        zfm[j] = send(unit(zj[2], yj[j], 1, 1), peer_z(-1))

    def pass_b(j):
        yp[j].wait_recv()
        yfp[j] = send(unit(zj[j], yj[1], 2, 1), peer_y(1))
        ym[j].wait_recv()
        yfm[j] = send(unit(zj[j], yj[2], 3, 1), peer_y(-1))

    a1p = send(unit(z, y, 0, 2), peer_y(1))
    b1p = send(unit(z, y, 2, 2), peer_z(1))
    a1m = send(unit(z, y, 0, 2), peer_y(-1))
    b1m = send(unit(z, y, 2, 2), peer_z(-1))
    spread_a(0)
    spread_b(0)
    yield
    a1p.wait_recv()
    a2p = send(unit(z, yj[1], 0, 1), peer_y(1))
    spread_a(1)
    b1p.wait_recv()
    b2p = send(unit(zj[1], y, 2, 1), peer_z(1))
    spread_b(1)
    yield
    a1m.wait_recv()
    a2m = send(unit(z, yj[2], 1, 1), peer_y(-1))
    spread_a(2)
    b1m.wait_recv()
    b2m = send(unit(zj[2], y, 3, 1), peer_z(-1))
    spread_b(2)
    yield
    pass_a(0)
    pass_b(0)
    yield
    a2p.wait_recv()
    a2m.wait_recv()
    spread_a(3)
    b2p.wait_recv()
    b2m.wait_recv()
    spread_b(3)
    yield
    for j in range(1, 4):
        pass_a(j)
        pass_b(j)
        zfp[j - 1].wait_recv()
        zfm[j - 1].wait_recv()
        on_a(j - 1)
        yield
    for copy in (zfp[3], zfm[3]):
        copy.wait_recv()
    on_a(3)
    for j in range(4):
        yfp[j].wait_recv()
        yfm[j].wait_recv()


def kernel(
    tokens, gain, w_query, w_keyval, w_out, cache, lengths, out,
    mine, raw, stat_y, stat_z, gain_col, normed, whole, w_rows, w_t, wo, acc, q_send, q_recv, kv_send, kv_recv,
    kv_t, keys, values, values_t, cosine, sine, scores, weights, queries, heads, heads_z, heads_all, acc_o, o_send, o_recv,
    send_sem, recv_sem, local_sem,
):
    x = lax.axis_index("gx")
    yz = lax.axis_index("yz")
    z, y, c = yz // 8, (yz // 2) % 4, yz % 2

    def device(xx, zz, yy, cc):
        return (xx, zz * 8 + yy * 2 + cc)

    peer_x = lambda d, dc=0: device(near(x, d), z, y, lax.rem(c + dc, 2))
    peer_y = lambda d: device(x, z, near(y, d), c)
    peer_z = lambda d, dc=0: device(x, near(z, d), y, lax.rem(c + dc, 2))
    sibling = device(x, z, y, 1 - c)

    barrier = pltpu.get_barrier_semaphore()
    peers = [sibling]
    for d in (1, 2, 3):
        peers += [peer_x(d), peer_x(d, 1), peer_z(d), peer_z(d, 1), peer_y(d)]
    for p in peers:
        pl.semaphore_signal(barrier, inc=1, device_id=p, device_id_type=MESH)

    locals_ = []

    def local(src, dst):
        copy = pltpu.make_async_copy(src, dst, local_sem.at[len(locals_)])
        copy.start()
        locals_.append(copy)
        return copy

    quarter = lambda k: pl.ds(pl.multiple_of(k * 144, 16), 144)
    own_mine = local(tokens.at[0], mine)
    slot_rows = pl.ds(pl.multiple_of(yz * 64, 64), 64)
    own_keys = local(cache.at[0, :, 0:256], keys.at[slot_rows, :])
    own_values = local(cache.at[0, :, 256:512], values.at[slot_rows, :])
    own_raw = local(tokens.at[0, quarter(z), :], raw.at[z])
    own_rows = local(w_query, w_rows)
    kv_rows16 = pl.ds(pl.multiple_of(512 + c * 16, 16), 16)
    own_kv = local(w_keyval, w_t.at[kv_rows16, :])
    own_wo = local(w_out, wo.at[c])

    own_mine.wait()
    v = mine[...].astype(F32)
    mean = jnp.sum(v, axis=0, keepdims=True) * (1.0 / 576)
    square = jnp.sum((v - mean) * (v - mean), axis=0, keepdims=True)
    row = lax.broadcasted_iota(jnp.int32, (8, 256), 0)

    def join(ref, count, size):
        means = [ref[k][0:1] for k in range(count)]
        mid = sum(means[1:], means[0]) * (1.0 / count)
        total = sum([ref[k][1:2] for k in range(1, count)], ref[0][1:2])
        for m in means:
            total = total + size * (m - mid) * (m - mid)
        return mid, total

    stat_y[y] = jnp.where(row == 0, mean, square)
    pl.semaphore_wait(barrier, len(peers))
    wires = Wires(send_sem, recv_sem)
    stat_1 = [wires(stat_y.at[y], stat_y.at[y], peer_y(d)) for d in (1, 3, 2)]
    first = [wires(tokens.at[0, quarter(near(z, d)), :], raw.at[z], peer_z(d)) for d in (1, 3, 2)]
    own_keys.wait()
    own_values.wait()

    def cache_unit(zz, yy, start, count):
        at = pl.ds(pl.multiple_of((zz * 8 + yy * 2 + c) * 64 + (start % 2) * 32, 32), count * 32)
        return keys.at[at, :] if start < 2 else values.at[at, :]

    cached = gather_plane(wires, cache_unit, peer_y, peer_z, y, z)
    next(cached)

    lane = lax.broadcasted_iota(jnp.int32, (16, 128), 1)
    sub = lax.broadcasted_iota(jnp.int32, (16, 128), 0)

    @pl.loop(0, 36)
    def _(k):
        g = (k // 9) * 288 + y * 72 + c * 36 + z * 9 + k % 9
        line = jnp.broadcast_to(gain[pl.ds(g // 8, 1), :], (16, 128))
        col = jnp.sum(jnp.where(lane == sub + (g % 8) * 16, line, 0.0), axis=1, keepdims=True)
        gain_col[pl.ds(pl.multiple_of(k * 16, 16), 16), :] = jnp.broadcast_to(col, (16, 256))

    for copy in stat_1:
        copy.wait_recv()
    mean, square = join(stat_y, 4, 576.0)
    me = z * 2 + c
    stat_z[me] = jnp.where(row == 0, mean, square)
    stat_2 = [wires(stat_z.at[me], stat_z.at[me], sibling)]
    for d in (1, 3, 2):
        for dc in (0, 1):
            stat_2.append(wires(stat_z.at[me], stat_z.at[me], peer_z(d, dc)))
    for copy in stat_2:
        copy.wait_recv()
    mean, square = join(stat_z, 8, 2304.0)
    scale = lax.rsqrt(square * (1.0 / 18432) + 1e-6)
    own_raw.wait()
    for copy in first:
        copy.wait_recv()
    for i in range(4):
        n = ((raw[i].astype(F32) - mean) * scale * gain_col[i * 144:(i + 1) * 144, :]).astype(BF16)
        for k in range(2):
            normed[i, k] = n[:, k * 128:(k + 1) * 128]

    spot = whole.at[x // 2, y, x % 2, c, z]
    second = []
    for d in (1, 3, 2, 0):
        for dc in (0, 1):
            if d or dc:
                second.append(wires(normed.at[near(x, d), lax.rem(c + dc, 2)], spot, peer_x(d, dc)))
    own_spot = local(normed.at[x, c], spot)
    next(cached)
    next(cached)
    next(cached)
    own_spot.wait()
    for copy in second:
        copy.wait_recv()

    def unit(zz, yy, start, count):
        if count == 2:
            return whole.at[start // 2, yy, :, :, zz]
        return whole.at[start // 2, yy, start % 2, :, zz]

    def project(half, yy, fresh_start):
        right = jnp.concatenate([whole[half, yy, b].reshape(1152, 128) for b in range(2)], axis=1)
        left = w_t[:, pl.ds(pl.multiple_of(yy * 1152, 128), 1152)]
        part = jnp.dot(left, right, preferred_element_type=F32)
        if fresh_start:
            acc[half] = part
        else:
            acc[half] += part

    yj = [y, near(y, -1), near(y, 1), near(y, 2)]
    gathered = gather_plane(wires, unit, peer_y, peer_z, y, z, lambda j: project(0, yj[j], j == 0))
    next(gathered)
    own_rows.wait()
    w_mine = pl.ds(pl.multiple_of(c * 256, 256), 256)

    @pl.loop(0, 18)
    def _(s):
        at = pl.ds(pl.multiple_of(s * 256, 256), 256)
        w_t[w_mine, at] = w_rows[at, :].T

    own_kv.wait()
    own_wo.wait()
    shared = [
        wires(w_t.at[w_mine, :], w_t.at[w_mine, :], sibling),
        wires(w_keyval, w_t.at[kv_rows16, :], sibling),
        wires(w_out, wo.at[c], sibling),
    ]
    next(gathered)
    next(gathered)
    for _ in cached:
        pass
    next(gathered)
    pair_rows = lambda ref: ref.reshape(16, 2, 64, 256).at[:, c]
    share_keys = wires(pair_rows(keys), pair_rows(keys), sibling)
    share_values = wires(pair_rows(values), pair_rows(values), sibling)
    freq = jnp.exp(
        lax.broadcasted_iota(jnp.int32, (128, 256), 0).astype(F32) * (-2.0 * math.log(10000.0) / HEAD)
    )
    angle = (lengths[0] + lax.broadcasted_iota(jnp.int32, (128, 256), 1)).astype(F32) * freq
    cosine[...] = jnp.cos(angle)
    sine[...] = jnp.sin(angle)
    for copy in shared[:2]:
        copy.wait_recv()
    for _ in gathered:
        pass

    @pl.loop(0, 4)
    def _(k):
        right = jnp.concatenate([whole[1, k, b].reshape(1152, 128) for b in range(2)], axis=1)
        left = w_t[:, pl.ds(pl.multiple_of(k * 1152, 128), 1152)]
        part = jnp.dot(left, right, preferred_element_type=F32)

        @pl.when(k == 0)
        def _():
            acc[1] = part

        @pl.when(k > 0)
        def _():
            acc[1] += part

    for b in range(4):
        lanes = slice((b % 2) * 128, (b % 2) * 128 + 128)
        kv_send[b] = acc[b // 2, 512:544, lanes]
        q_send[b] = acc[b // 2, 0:512, lanes].astype(BF16)
    third, fourth = [], []
    for d in (1, 3, 2):
        third.append(wires(kv_send.at[near(x, d)], kv_recv.at[x], peer_x(d)))
    for d in (1, 3, 2):
        fourth.append(wires(q_send.at[near(x, d)], q_recv.at[x], peer_x(d)))
    for copy in third:
        copy.wait_recv()
    total = kv_send[x]
    for d in (1, 2, 3):
        total = total + kv_recv[near(x, d)]
    kv_block = lambda zz, yy: kv_t.at[c, pl.ds(pl.multiple_of((zz * 4 + yy) * 32, 32), 32), :]
    kv_t[c, pl.ds(pl.multiple_of((z * 4 + y) * 32, 32), 32), :] = total.astype(BF16)
    kv_y = [wires(kv_block(z, y), kv_block(z, y), peer_y(d)) for d in (1, 3, 2)]
    for copy in kv_y:
        copy.wait_recv()
    kv_rows = kv_t.at[c, pl.ds(pl.multiple_of(z * 128, 128), 128), :]
    kv_z = [wires(kv_rows, kv_rows, sibling)]
    for d in (1, 3, 2):
        for dc in (0, 1):
            kv_z.append(wires(kv_rows, kv_rows, peer_z(d, dc)))
    share_values.wait_recv()

    @pl.loop(0, 8)
    def _(s):
        at = pl.ds(pl.multiple_of(s * 256, 256), 256)
        values_t[:, at] = values[at, :].T

    share_keys.wait_recv()

    for copy in fourth:
        copy.wait_recv()
    query = q_send[x].astype(F32)
    for d in (1, 2, 3):
        query = query + q_recv[near(x, d)].astype(F32)
    half_lanes = pl.ds(pl.multiple_of(c * 128, 128), 128)
    cos_q, sin_q = cosine[:, half_lanes], sine[:, half_lanes]
    for h in range(2):
        u, w = query[h * 256:h * 256 + 128], query[h * 256 + 128:h * 256 + 256]
        queries[0:128, h * 128:(h + 1) * 128] = (u * cos_q - w * sin_q).astype(BF16)
        queries[128:256, h * 128:(h + 1) * 128] = (w * cos_q + u * sin_q).astype(BF16)
    inv = 1.0 / math.sqrt(HEAD)

    def fold(s, f):
        return f(s.reshape(s.shape[0] // 8, 8, 256), axis=0)

    def cached_scores(k, top):
        at = pl.ds(pl.multiple_of(k * 256, 256), 256)
        s = jnp.dot(keys[at, :], queries[...], preferred_element_type=F32) * inv
        slot = k * 256 + lax.broadcasted_iota(jnp.int32, (256, 256), 0)
        s = jnp.where(slot < lengths[0], s, -1e30)
        scores[at, :] = s
        return jnp.maximum(top, fold(s, jnp.max))

    top = lax.fori_loop(0, 8, cached_scores, jnp.full((8, 256), -1e30, F32))
    for copy in kv_z:
        copy.wait_recv()
    kv = jnp.concatenate([kv_t[0], kv_t[1]], axis=1)
    u, w = kv[0:128].astype(F32), kv[128:256].astype(F32)
    fresh = jnp.concatenate([u * cosine[...] - w * sine[...], w * cosine[...] + u * sine[...]], axis=0).astype(BF16)
    s = lax.dot_general(fresh, queries[...], LEFT, preferred_element_type=F32) * inv
    t = c * 128 + lax.rem(lax.broadcasted_iota(jnp.int32, (256, 256), 1), 128)
    t2 = lax.broadcasted_iota(jnp.int32, (256, 256), 0)
    s = jnp.where(t2 <= t, s, -1e30)
    scores[2048:2304, :] = s
    top = jnp.max(jnp.maximum(top, fold(s, jnp.max)), axis=0, keepdims=True)

    def exponentials(k, total):
        at = pl.ds(pl.multiple_of(k * 256, 256), 256)
        p = jnp.exp(scores[at, :] - top)
        weights[at, :] = p.astype(BF16)
        return total + fold(p, jnp.sum)

    total = jnp.sum(lax.fori_loop(0, 9, exponentials, jnp.zeros((8, 256), F32)), axis=0, keepdims=True)
    summed = jnp.dot(values_t[...], weights[0:2048, :], preferred_element_type=F32)
    summed += jnp.dot(kv[256:512], weights[2048:2304, :], preferred_element_type=F32)
    done = (summed / total).astype(BF16)
    heads[0] = done[:, 0:128]
    heads[1] = done[:, 128:256]

    fifth = []
    for d in (1, 3, 2):
        rows = pl.ds(pl.multiple_of(near(z, d) * 64, 64), 64)
        fifth.append(wires(heads.at[:, rows, :], heads_z.at[z], peer_z(d)))
    own = local(heads.at[:, pl.ds(pl.multiple_of(z * 64, 64), 64), :], heads_z.at[z])
    own.wait()
    for copy in fifth:
        copy.wait_recv()
    head_spot = heads_all.at[x // 2, y, x % 2, :, z]
    sixth = [wires(heads_z.at[near(x, d)], head_spot, peer_x(d)) for d in (1, 3, 2)]
    own = local(heads_z.at[x], head_spot)
    own.wait()
    for copy in sixth:
        copy.wait_recv()

    def head_unit(zz, yy, start, count):
        if count == 2:
            return heads_all.at[start // 2, yy, :, :, zz]
        return heads_all.at[start // 2, yy, start % 2, :, zz]

    shared[2].wait_recv()

    def project_out(half, yy, fresh_start):
        right = jnp.concatenate([heads_all[half, yy, b].reshape(512, 128) for b in range(2)], axis=1)
        for k in range(2):
            left = wo[k, :, pl.ds(pl.multiple_of(yy * 512, 128), 512)]
            part = jnp.dot(left, right, preferred_element_type=F32)
            if fresh_start:
                acc_o[k] = part
            else:
                acc_o[k] += part

    for _ in gather_plane(wires, head_unit, peer_y, peer_z, y, z, lambda j: project_out(0, yj[j], j == 0)):
        pass
    right = jnp.concatenate([heads_all[1, :, b].reshape(2048, 128) for b in range(2)], axis=1)
    for k in range(2):
        for b in range(2):
            o_send[b, k] = acc_o[k][:, b * 128:(b + 1) * 128].astype(BF16)
        part = jnp.dot(wo[k], right, preferred_element_type=F32)
        for b in range(2):
            o_send[2 + b, k] = part[:, b * 128:(b + 1) * 128].astype(BF16)
    last = []
    for d in (2, 1, 3, 0):
        for dc in (0, 1):
            if d or dc:
                last.append(wires(o_send.at[near(x, d), lax.rem(c + dc, 2)], o_recv.at[x, c], peer_x(d, dc)))
    own = local(o_send.at[x, c], o_recv.at[x, c])
    own.wait()
    for copy in last:
        copy.wait_recv()
    for k in range(2):
        total = o_recv[0, k].astype(F32)
        for xx in (1, 2, 3):
            total = total + o_recv[xx, k].astype(F32)
        out[0, :, k * 128:(k + 1) * 128] = total.astype(BF16)

    for copy in wires.all:
        copy.wait_send()


def body(tokens, gain, w_query, w_keyval, w_out, cache, lengths):
    hbm = pl.BlockSpec(memory_space=pl.ANY)
    vmem = pl.BlockSpec(memory_space=pltpu.VMEM)
    smem = pl.BlockSpec(memory_space=pltpu.SMEM)
    out = pl.pallas_call(
        kernel,
        out_shape=jax.ShapeDtypeStruct((1, 576, 256), BF16),
        in_specs=[hbm, vmem, hbm, hbm, hbm, hbm, smem],
        out_specs=vmem,
        scratch_shapes=[
            pltpu.VMEM((576, 256), BF16),
            pltpu.VMEM((4, 144, 256), BF16),
            pltpu.VMEM((4, 8, 256), F32),
            pltpu.VMEM((8, 8, 256), F32),
            pltpu.VMEM((576, 256), F32),
            pltpu.VMEM((4, 2, 144, 128), BF16),
            pltpu.VMEM((2, 4, 2, 2, 4, 144, 128), BF16),
            pltpu.VMEM((4608, 256), BF16),
            pltpu.VMEM((544, 4608), BF16),
            pltpu.VMEM((2, 576, 2048), BF16),
            pltpu.VMEM((2, 544, 256), F32),
            pltpu.VMEM((4, 512, 128), BF16),
            pltpu.VMEM((4, 512, 128), BF16),
            pltpu.VMEM((4, 32, 128), F32),
            pltpu.VMEM((4, 32, 128), F32),
            pltpu.VMEM((2, 512, 128), BF16),
            pltpu.VMEM((2048, 256), BF16),
            pltpu.VMEM((2048, 256), BF16),
            pltpu.VMEM((256, 2048), BF16),
            pltpu.VMEM((128, 256), F32),
            pltpu.VMEM((128, 256), F32),
            pltpu.VMEM((2304, 256), F32),
            pltpu.VMEM((2304, 256), BF16),
            pltpu.VMEM((256, 256), BF16),
            pltpu.VMEM((2, 256, 128), BF16),
            pltpu.VMEM((4, 2, 64, 128), BF16),
            pltpu.VMEM((2, 4, 2, 2, 4, 64, 128), BF16),
            pltpu.VMEM((2, 576, 256), F32),
            pltpu.VMEM((4, 2, 576, 128), BF16),
            pltpu.VMEM((4, 2, 576, 128), BF16),
            pltpu.SemaphoreType.DMA((200,)),
            pltpu.SemaphoreType.DMA((200,)),
            pltpu.SemaphoreType.DMA((16,)),
        ],
        compiler_params=pltpu.CompilerParams(
            collective_id=0, has_side_effects=True, vmem_limit_bytes=56 * 1024 * 1024
        ),
    )(
        jnp.swapaxes(tokens, 1, 2), gain.reshape(144, 128), w_query, w_keyval.T, w_out.T, cache, lengths
    )
    return jnp.swapaxes(out, 1, 2)


def solution(mesh):
    return jax.shard_map(
        body,
        mesh=mesh,
        in_specs=(
            P("gx", None, "yz"),
            P(),
            P("gx", "yz"),
            P("gx", "yz"),
            P("gx", "yz"),
            P("gx", "yz", None),
            P("gx"),
        ),
        out_specs=P("gx", None, "yz"),
        check_vma=False,
    )
```

time: 369 us -> 120 us (0.33)
  waiting for transfers between devices: 279 us -> 0 us
  Pallas kernels: 0 us -> 117 us
  blocking collectives: 37.4 us -> 0 us
  matrix products: 27.5 us -> 0 us
  between operations: 13.9 us -> 0.66 us
  other arithmetic: 10.9 us -> 0 us
    all_gather x5 -> x0, waiting for transfers between devices: 277 us -> none  [the longest x1 87.2 us: body(): lax.all_gather(w_out, 'gx', axis=0, tiled=True)]
    pallas_call x0 -> x1, Pallas kernels: none -> 117 us  [body(): pl.pallas_call(kernel, out_shape=jax.ShapeDtypeStruct((1, 576, 256), BF16...]
    all_gather x2 -> x0, blocking collectives: 37.4 us -> none  [the longest x1 24.7 us: body(): lax.all_gather(pair_part.astype(jnp.bfloat16).reshape(rows, span, pair_co...]
    dot_general x7 -> x0, matrix products: 27.5 us -> none  [the longest x1 11.4 us: body(): jnp.dot(left, lax.all_gather(w_query, 'gx', axis=0, tiled=True), preferre...]
    reduce_sum x4 -> x0, other arithmetic: 10.3 us -> none  [the longest x1 7.01 us: layer_norm(): mean = jnp.mean(values, axis=-1, keepdims=True)]
  transfers between devices with their start and end apart: 5 -> 0, of which waited for: 5 -> 0; matrix products, arithmetic and copies ran while one was open for 8% -> 0% of each run, Pallas kernels for 0% -> 0%
where the time goes in v2:
time: 120 us
  Pallas kernels  117 us (98%)
  local copies, waits for them, and re-layouts  1.69 us (1%)
    pallas_call x1, Pallas kernels, body(): pl.pallas_call(kernel, out_shape=jax.ShapeDtypeStruct((1, 576, 256), BF16...  117 us

profile of v2, /device:TPU:1, one launch (start us, length us, event | category | flops | bytes accessed | tf_op | source)
XLA Modules:
  0.0 119.8 jit_solution(2873506670968403214)
XLA Ops:
  0.7 117.4 %shard_map.73 = bf16[1,576,256]{2,1,0:T(8,128)(2,1)} custom-call(bf16[1,576,256]{2,1,0:T(8,128)(2,1)} %bitcast.7, f32[144,128]{1,0:T(8,128)} %bitcast.9, bf16[4608,256]{1,0:T(8,128)(2,1)} %w_query.1, bf16[16,4608]{1,0:T(8,128)(2,1)} %bitcast.8, bf16[576,2048]{1,0:T(8,128)(2,1)} %bitcast.5, bf16[1,64,512]{2,1,0:T(8,128)(2,1)} %cache.1, s32[1]{0:T(128)S(6)} %copy.9.lengths), custom_call_target="tpu_custom_call" | custom-call | tf_op jit(solution)/shard_map/pallas_call | solution.py:443
  118.1 1.7 %copy.10 = bf16[1,256,576]{1,2,0:T(8,128)(2,1)} copy(bf16[1,256,576]{1,2,0:T(8,128)(2,1)} %bitcast.6) | data formatting | bytes 589824

commit v3 on v2

--- a/solution.py
+++ b/solution.py
@@ -34,7 +34,7 @@
     return lax.rem(v + d + 4, 4)
 
 
-def gather_plane(wires, unit, peer_y, peer_z, y, z, on_a=lambda j: None):
+def gather_plane(wires, unit, peer_y, peer_z, y, z, on_a=lambda j: None, on_b=lambda j: None, direct=False):
     yj = [y, near(y, -1), near(y, 1), near(y, 2)]
     zj = [z, near(z, -1), near(z, 1), near(z, 2)]
 
@@ -70,31 +70,41 @@
     b1m = send(unit(z, y, 2, 2), peer_z(-1))
     spread_a(0)
     spread_b(0)
+    if direct:
+        a2p = send(unit(z, y, 0, 2), peer_y(2))
+        b2p = send(unit(z, y, 2, 2), peer_z(2))
     yield
     a1p.wait_recv()
-    a2p = send(unit(z, yj[1], 0, 1), peer_y(1))
+    if not direct:
+        a2p = send(unit(z, yj[1], 0, 1), peer_y(1))
     spread_a(1)
     b1p.wait_recv()
-    b2p = send(unit(zj[1], y, 2, 1), peer_z(1))
+    if not direct:
+        b2p = send(unit(zj[1], y, 2, 1), peer_z(1))
     spread_b(1)
     yield
     a1m.wait_recv()
-    a2m = send(unit(z, yj[2], 1, 1), peer_y(-1))
+    a2 = [a2p]
+    if not direct:
+        a2.append(send(unit(z, yj[2], 1, 1), peer_y(-1)))
     spread_a(2)
     b1m.wait_recv()
-    b2m = send(unit(zj[2], y, 3, 1), peer_z(-1))
+    b2 = [b2p]
+    if not direct:
+        b2.append(send(unit(zj[2], y, 3, 1), peer_z(-1)))
     spread_b(2)
     yield
     pass_a(0)
     pass_b(0)
     yield
-    a2p.wait_recv()
-    a2m.wait_recv()
+    for copy in a2:
+        copy.wait_recv()
     spread_a(3)
-    b2p.wait_recv()
-    b2m.wait_recv()
+    for copy in b2:
+        copy.wait_recv()
     spread_b(3)
     yield
+    on_b(0)
     for j in range(1, 4):
         pass_a(j)
         pass_b(j)
@@ -102,19 +112,89 @@
         zfm[j - 1].wait_recv()
         on_a(j - 1)
         yield
+    on_b(1)
+    on_b(2)
     for copy in (zfp[3], zfm[3]):
         copy.wait_recv()
     on_a(3)
     for j in range(4):
         yfp[j].wait_recv()
         yfm[j].wait_recv()
+    on_b(3)
+
+
+def gather_direct(wires, unit, peer_y, peer_z, y, z, on_a=lambda j: None, on_b=lambda j: None):
+    yj = [y, near(y, -1), near(y, 1), near(y, 2)]
+    zj = [z, near(z, -1), near(z, 1), near(z, 2)]
+    ways = (1, -1, 2)
+
+    def send(ref, peer):
+        return [wires(ref, ref, peer(d)) for d in ways]
+
+    own_a, own_b = unit(z, y, 0, 2), unit(z, y, 2, 2)
+    a1, b1 = send(own_a, peer_y), send(own_b, peer_z)
+    a2, b2 = [send(own_a, peer_z)], [send(own_b, peer_y)]
+    yield
+    for j in range(3):
+        a1[j].wait_recv()
+        a2.append(send(unit(z, yj[j + 1], 0, 2), peer_z))
+        b1[j].wait_recv()
+        b2.append(send(unit(zj[j + 1], y, 2, 2), peer_y))
+        yield
+    on_b(0)
+    for j in range(4):
+        for copy in a2[j]:
+            copy.wait_recv()
+        on_a(j)
+        yield
+    for j in (1, 2, 3):
+        for k in range(4):
+            b2[k][j - 1].wait_recv()
+        on_b(j)
+
+
+def gather_lines(wires, unit, peer_y, peer_z, y, z):
+    yj = [y, near(y, -1), near(y, 1), near(y, 2)]
+    zj = [z, near(z, -1), near(z, 1), near(z, 2)]
+
+    def send(ref, target):
+        return wires(ref, ref, target)
+
+    def spread(j):
+        ref = unit(zj[j], y, None)
+        return [send(ref, peer_y(1)), send(ref, peer_y(-1))]
+
+    def hand_on(j, pair):
+        pair[0].wait_recv()
+        first = send(unit(zj[j], yj[1], 0), peer_y(1))
+        pair[1].wait_recv()
+        return [first, send(unit(zj[j], yj[2], 1), peer_y(-1))]
+
+    own = unit(z, y, None)
+    along = [send(own, peer_z(d)) for d in (1, -1, 2)]
+    near_y = [spread(0)]
+    yield
+    for j in (1, 2):
+        along[j - 1].wait_recv()
+        near_y.append(spread(j))
+    far_y = [hand_on(0, near_y[0])]
+    yield
+    along[2].wait_recv()
+    near_y.append(spread(3))
+    for j in (1, 2, 3):
+        yield
+        far_y.append(hand_on(j, near_y[j]))
+    yield
+    for pair in far_y:
+        for copy in pair:
+            copy.wait_recv()
 
 
 def kernel(
     tokens, gain, w_query, w_keyval, w_out, cache, lengths, out,
-    mine, raw, stat_y, stat_z, gain_col, normed, whole, w_rows, w_t, wo, acc, q_send, q_recv, kv_send, kv_recv,
-    kv_t, keys, values, values_t, cosine, sine, scores, weights, queries, heads, heads_z, heads_all, acc_o, o_send, o_recv,
-    send_sem, recv_sem, local_sem,
+    mine, raw, stat_y, stat_z, stat_x, gain_col, whole, w_rows, w_t, wo, acc, q_send, q_recv, kv_send, kv_recv,
+    kv_t, slots, values_t, cosine, sine, scores, weights, queries, heads, heads_all, acc_o, o_send, o_recv,
+    send_sem, recv_sem, local_sem, block_send, block_recv, swap_sem,
 ):
     x = lax.axis_index("gx")
     yz = lax.axis_index("yz")
@@ -132,6 +212,8 @@
     peers = [sibling]
     for d in (1, 2, 3):
         peers += [peer_x(d), peer_x(d, 1), peer_z(d), peer_z(d, 1), peer_y(d)]
+    twin = device(3 - x, 3 - z, y, c)
+    peers.append(twin)
     for p in peers:
         pl.semaphore_signal(barrier, inc=1, device_id=p, device_id_type=MESH)
 
@@ -146,13 +228,50 @@
     quarter = lambda k: pl.ds(pl.multiple_of(k * 144, 16), 144)
     own_mine = local(tokens.at[0], mine)
     slot_rows = pl.ds(pl.multiple_of(yz * 64, 64), 64)
-    own_keys = local(cache.at[0, :, 0:256], keys.at[slot_rows, :])
-    own_values = local(cache.at[0, :, 256:512], values.at[slot_rows, :])
+    own_slots = local(cache.at[0], slots.at[slot_rows, :])
     own_raw = local(tokens.at[0, quarter(z), :], raw.at[z])
     own_rows = local(w_query, w_rows)
     kv_rows16 = pl.ds(pl.multiple_of(512 + c * 16, 16), 16)
     own_kv = local(w_keyval, w_t.at[kv_rows16, :])
-    own_wo = local(w_out, wo.at[c])
+    pair = x // 2
+    partner = device(x + 1 - 2 * (x % 2), z, y, c)
+    wo_lanes = pl.ds(pl.multiple_of((x % 2) * 2048, 128), 2048)
+    wo_other = pl.ds(pl.multiple_of((1 - x % 2) * 2048, 128), 2048)
+    own_wo = local(w_out, wo.at[c, :, wo_lanes])
+    wo_rows = lambda k: pl.ds(k * 48, 48)
+
+    def lend(k):
+        return wires(w_out.at[wo_rows(k), :], wo.at[c, wo_rows(k), wo_lanes], partner)
+
+
+    pl.semaphore_wait(barrier, len(peers))
+    wires = Wires(send_sem, recv_sem)
+    first = [wires(tokens.at[0, quarter(near(z, d)), :], raw.at[z], peer_z(d)) for d in (1, 3, 2)]
+
+    spot = whole.at[x // 2, y, x % 2, c, z]
+    half_lanes = lambda k: pl.ds(pl.multiple_of(k * 128, 128), 128)
+
+    def block(e, dc):
+        i, cc = near(z, e), lax.rem(c + dc, 2)
+        return pltpu.make_async_remote_copy(
+            src_ref=raw.at[i, :, half_lanes(cc)], dst_ref=spot, send_sem=block_send.at[e * 2 + dc],
+            recv_sem=block_recv.at[x * 2 + c], device_id=device(i, z, y, cc), device_id_type=MESH,
+        )
+
+    def start_block(e):
+        @pl.when(near(z, e) == x)
+        def _():
+            pltpu.make_async_copy(raw.at[x, :, half_lanes(c)], spot, block_recv.at[x * 2 + c]).start()
+
+        @pl.when(near(z, e) != x)
+        def _():
+            block(e, 0).start()
+
+        block(e, 1).start()
+
+    own_raw.wait()
+    start_block(0)
+    lent = [lend(k) for k in range(0)]
 
     own_mine.wait()
     v = mine[...].astype(F32)
@@ -169,64 +288,66 @@
         return mid, total
 
     stat_y[y] = jnp.where(row == 0, mean, square)
-    pl.semaphore_wait(barrier, len(peers))
-    wires = Wires(send_sem, recv_sem)
     stat_1 = [wires(stat_y.at[y], stat_y.at[y], peer_y(d)) for d in (1, 3, 2)]
-    first = [wires(tokens.at[0, quarter(near(z, d)), :], raw.at[z], peer_z(d)) for d in (1, 3, 2)]
-    own_keys.wait()
-    own_values.wait()
-
-    def cache_unit(zz, yy, start, count):
-        at = pl.ds(pl.multiple_of((zz * 8 + yy * 2 + c) * 64 + (start % 2) * 32, 32), count * 32)
-        return keys.at[at, :] if start < 2 else values.at[at, :]
-
-    cached = gather_plane(wires, cache_unit, peer_y, peer_z, y, z)
+    own_slots.wait()
+
+    def cache_unit(zz, yy, part):
+        at = (zz * 8 + yy * 2 + c) * 64 + (0 if part is None else part * 32)
+        return slots.at[pl.ds(pl.multiple_of(at, 32), 64 if part is None else 32), :]
+
+    cached = gather_lines(wires, cache_unit, peer_y, peer_z, y, z)
     next(cached)
 
     lane = lax.broadcasted_iota(jnp.int32, (16, 128), 1)
     sub = lax.broadcasted_iota(jnp.int32, (16, 128), 0)
 
-    @pl.loop(0, 36)
-    def _(k):
-        g = (k // 9) * 288 + y * 72 + c * 36 + z * 9 + k % 9
+    for k in range(18):
+        g = x * 288 + y * 72 + (k // 9) * 36 + z * 9 + k % 9
         line = jnp.broadcast_to(gain[pl.ds(g // 8, 1), :], (16, 128))
         col = jnp.sum(jnp.where(lane == sub + (g % 8) * 16, line, 0.0), axis=1, keepdims=True)
-        gain_col[pl.ds(pl.multiple_of(k * 16, 16), 16), :] = jnp.broadcast_to(col, (16, 256))
+        gain_col[k * 16:(k + 1) * 16, :] = jnp.broadcast_to(col, (16, 128))
 
     for copy in stat_1:
         copy.wait_recv()
     mean, square = join(stat_y, 4, 576.0)
     me = z * 2 + c
     stat_z[me] = jnp.where(row == 0, mean, square)
-    stat_2 = [wires(stat_z.at[me], stat_z.at[me], sibling)]
+    stat_2 = []
     for d in (1, 3, 2):
         for dc in (0, 1):
             stat_2.append(wires(stat_z.at[me], stat_z.at[me], peer_z(d, dc)))
+    stat_2.append(wires(stat_z.at[me], stat_z.at[me], sibling))
+    first[0].wait_recv()
+    start_block(3)
+    first[1].wait_recv()
+    start_block(1)
+    next(cached)
     for copy in stat_2:
         copy.wait_recv()
     mean, square = join(stat_z, 8, 2304.0)
-    scale = lax.rsqrt(square * (1.0 / 18432) + 1e-6)
-    own_raw.wait()
-    for copy in first:
-        copy.wait_recv()
-    for i in range(4):
-        n = ((raw[i].astype(F32) - mean) * scale * gain_col[i * 144:(i + 1) * 144, :]).astype(BF16)
-        for k in range(2):
-            normed[i, k] = n[:, k * 128:(k + 1) * 128]
-
-    spot = whole.at[x // 2, y, x % 2, c, z]
-    second = []
-    for d in (1, 3, 2, 0):
-        for dc in (0, 1):
-            if d or dc:
-                second.append(wires(normed.at[near(x, d), lax.rem(c + dc, 2)], spot, peer_x(d, dc)))
-    own_spot = local(normed.at[x, c], spot)
+    stat_x[x] = jnp.where(row == 0, mean, lax.rsqrt(square * (1.0 / 18432) + 1e-6))
+    stat_3 = [wires(stat_x.at[x], stat_x.at[x], peer_x(d)) for d in (1, 3, 2)]
+    first[2].wait_recv()
+    start_block(2)
     next(cached)
     next(cached)
-    next(cached)
-    own_spot.wait()
-    for copy in second:
-        copy.wait_recv()
+    for k in range(8):
+        pltpu.make_async_copy(raw.at[0, :, 0:128], whole.at[k // 4, y, (k // 2) % 2, k % 2, z], block_recv.at[k]).wait()
+    for copy in stat_3:
+        copy.wait_recv()
+    for b in range(4):
+        norm = stat_x[b, :, half_lanes(c)]
+        for k in range(2):
+            v = whole[b // 2, y, b % 2, k, z].astype(F32)
+            v = (v - norm[0:1]) * norm[1:2] * gain_col[k * 144:(k + 1) * 144, :]
+            whole[b // 2, y, b % 2, k, z] = v.astype(BF16)
+    for e in range(4):
+        @pl.when(near(z, e) != x)
+        def _():
+            block(e, 0).wait_send()
+
+        block(e, 1).wait_send()
+
 
     def unit(zz, yy, start, count):
         if count == 2:
@@ -243,7 +364,10 @@
             acc[half] += part
 
     yj = [y, near(y, -1), near(y, 1), near(y, 2)]
-    gathered = gather_plane(wires, unit, peer_y, peer_z, y, z, lambda j: project(0, yj[j], j == 0))
+    lent += [lend(k) for k in range(0, 7)]
+    gathered = gather_plane(wires, unit, peer_y, peer_z, y, z, lambda j: project(0, yj[j], j == 0), lambda j: project(1, yj[j], j == 0))
+    next(gathered)
+    next(gathered)
     next(gathered)
     own_rows.wait()
     w_mine = pl.ds(pl.multiple_of(c * 256, 256), 256)
@@ -258,41 +382,26 @@
     shared = [
         wires(w_t.at[w_mine, :], w_t.at[w_mine, :], sibling),
         wires(w_keyval, w_t.at[kv_rows16, :], sibling),
-        wires(w_out, wo.at[c], sibling),
+        wires(w_out, wo.at[c, :, wo_lanes], sibling),
     ]
     next(gathered)
+    next(cached)
+    next(cached)
+    for copy in shared[:2]:
+        copy.wait_recv()
     next(gathered)
     for _ in cached:
         pass
-    next(gathered)
-    pair_rows = lambda ref: ref.reshape(16, 2, 64, 256).at[:, c]
-    share_keys = wires(pair_rows(keys), pair_rows(keys), sibling)
-    share_values = wires(pair_rows(values), pair_rows(values), sibling)
+    share = slots.reshape(16, 2, 64, 512).at[:, c]
+    share_slots = wires(share, share, sibling)
     freq = jnp.exp(
         lax.broadcasted_iota(jnp.int32, (128, 256), 0).astype(F32) * (-2.0 * math.log(10000.0) / HEAD)
     )
     angle = (lengths[0] + lax.broadcasted_iota(jnp.int32, (128, 256), 1)).astype(F32) * freq
     cosine[...] = jnp.cos(angle)
     sine[...] = jnp.sin(angle)
-    for copy in shared[:2]:
-        copy.wait_recv()
     for _ in gathered:
         pass
-
-    @pl.loop(0, 4)
-    def _(k):
-        right = jnp.concatenate([whole[1, k, b].reshape(1152, 128) for b in range(2)], axis=1)
-        left = w_t[:, pl.ds(pl.multiple_of(k * 1152, 128), 1152)]
-        part = jnp.dot(left, right, preferred_element_type=F32)
-
-        @pl.when(k == 0)
-        def _():
-            acc[1] = part
-
-        @pl.when(k > 0)
-        def _():
-            acc[1] += part
-
     for b in range(4):
         lanes = slice((b % 2) * 128, (b % 2) * 128 + 128)
         kv_send[b] = acc[b // 2, 512:544, lanes]
@@ -317,22 +426,21 @@
     for d in (1, 3, 2):
         for dc in (0, 1):
             kv_z.append(wires(kv_rows, kv_rows, peer_z(d, dc)))
-    share_values.wait_recv()
+    share_slots.wait_recv()
 
     @pl.loop(0, 8)
     def _(s):
         at = pl.ds(pl.multiple_of(s * 256, 256), 256)
-        values_t[:, at] = values[at, :].T
-
-    share_keys.wait_recv()
+        values_t[:, at] = slots[at, 256:512].T
+
 
     for copy in fourth:
         copy.wait_recv()
+    lent += [lend(k) for k in range(7, 12)]
     query = q_send[x].astype(F32)
     for d in (1, 2, 3):
         query = query + q_recv[near(x, d)].astype(F32)
-    half_lanes = pl.ds(pl.multiple_of(c * 128, 128), 128)
-    cos_q, sin_q = cosine[:, half_lanes], sine[:, half_lanes]
+    cos_q, sin_q = cosine[:, half_lanes(c)], sine[:, half_lanes(c)]
     for h in range(2):
         u, w = query[h * 256:h * 256 + 128], query[h * 256 + 128:h * 256 + 256]
         queries[0:128, h * 128:(h + 1) * 128] = (u * cos_q - w * sin_q).astype(BF16)
@@ -344,7 +452,7 @@
 
     def cached_scores(k, top):
         at = pl.ds(pl.multiple_of(k * 256, 256), 256)
-        s = jnp.dot(keys[at, :], queries[...], preferred_element_type=F32) * inv
+        s = jnp.dot(slots[at, 0:256], queries[...], preferred_element_type=F32) * inv
         slot = k * 256 + lax.broadcasted_iota(jnp.int32, (256, 256), 0)
         s = jnp.where(slot < lengths[0], s, -1e30)
         scores[at, :] = s
@@ -376,61 +484,69 @@
     heads[0] = done[:, 0:128]
     heads[1] = done[:, 128:256]
 
-    fifth = []
-    for d in (1, 3, 2):
-        rows = pl.ds(pl.multiple_of(near(z, d) * 64, 64), 64)
-        fifth.append(wires(heads.at[:, rows, :], heads_z.at[z], peer_z(d)))
-    own = local(heads.at[:, pl.ds(pl.multiple_of(z * 64, 64), 64), :], heads_z.at[z])
-    own.wait()
-    for copy in fifth:
-        copy.wait_recv()
-    head_spot = heads_all.at[x // 2, y, x % 2, :, z]
-    sixth = [wires(heads_z.at[near(x, d)], head_spot, peer_x(d)) for d in (1, 3, 2)]
-    own = local(heads_z.at[x], head_spot)
-    own.wait()
-    for copy in sixth:
-        copy.wait_recv()
+    stays = z // 2 == pair
+    swap = pltpu.make_async_remote_copy(
+        src_ref=heads, dst_ref=heads_all.at[y, 3 - z], send_sem=swap_sem.at[0], recv_sem=swap_sem.at[1],
+        device_id=twin, device_id_type=MESH,
+    )
+    keep = pltpu.make_async_copy(heads, heads_all.at[y, z], swap_sem.at[1])
+    pl.when(stays)(keep.start)
+    pl.when(jnp.logical_not(stays))(swap.start)
+    passed = []
+    for k in range(7):
+        lent[k].wait_recv()
+        passed.append(wires(wo.at[c, wo_rows(k), wo_other], wo.at[c, wo_rows(k), wo_other], sibling))
+    shared[2].wait_recv()
+    keep.wait()
+    pl.when(jnp.logical_not(stays))(swap.wait_send)
 
     def head_unit(zz, yy, start, count):
-        if count == 2:
-            return heads_all.at[start // 2, yy, :, :, zz]
-        return heads_all.at[start // 2, yy, start % 2, :, zz]
-
-    shared[2].wait_recv()
-
-    def project_out(half, yy, fresh_start):
-        right = jnp.concatenate([heads_all[half, yy, b].reshape(512, 128) for b in range(2)], axis=1)
+        return heads_all.at[yy, zz, start // 2, (start % 2) * 128:(start % 2 + count) * 128, :]
+
+    def project_out(h, yy, fresh_start):
+        rights, lanes = [], []
+        for j in range(2):
+            block = 2 * pair + j
+            rights.append(jnp.concatenate([heads_all[yy, block, h], heads_all[yy, 3 - block, h]], axis=1))
+            lanes.append(pl.ds(pl.multiple_of(j * 2048 + yy * 512 + h * 256, 128), 256))
+        right = jnp.concatenate(rights, axis=0)
         for k in range(2):
-            left = wo[k, :, pl.ds(pl.multiple_of(yy * 512, 128), 512)]
+            left = jnp.concatenate([wo[k, :, lanes[0]], wo[k, :, lanes[1]]], axis=1)
             part = jnp.dot(left, right, preferred_element_type=F32)
             if fresh_start:
                 acc_o[k] = part
             else:
                 acc_o[k] += part
 
-    for _ in gather_plane(wires, head_unit, peer_y, peer_z, y, z, lambda j: project_out(0, yj[j], j == 0)):
+    begun = []
+
+    def absorb(h, j):
+        if not begun:
+            for copy in passed:
+                copy.wait_recv()
+        project_out(h, yj[j], not begun)
+        begun.append(j)
+
+    heads_gather = gather_plane(wires, head_unit, peer_y, peer_z, y, z, lambda j: absorb(0, j), lambda j: absorb(1, j), direct=True)
+    for step in range(4):
+        next(heads_gather)
+    for k in range(7, 12):
+        lent[k].wait_recv()
+        passed.append(wires(wo.at[c, wo_rows(k), wo_other], wo.at[c, wo_rows(k), wo_other], sibling))
+    for _ in heads_gather:
         pass
-    right = jnp.concatenate([heads_all[1, :, b].reshape(2048, 128) for b in range(2)], axis=1)
     for k in range(2):
-        for b in range(2):
-            o_send[b, k] = acc_o[k][:, b * 128:(b + 1) * 128].astype(BF16)
-        part = jnp.dot(wo[k], right, preferred_element_type=F32)
-        for b in range(2):
-            o_send[2 + b, k] = part[:, b * 128:(b + 1) * 128].astype(BF16)
-    last = []
-    for d in (2, 1, 3, 0):
-        for dc in (0, 1):
-            if d or dc:
-                last.append(wires(o_send.at[near(x, d), lax.rem(c + dc, 2)], o_recv.at[x, c], peer_x(d, dc)))
-    own = local(o_send.at[x, c], o_recv.at[x, c])
-    own.wait()
+        o_send[0, k] = acc_o[k, :, 128:256].astype(BF16)
+    last = [
+        wires(o_send.at[0, lax.rem(c + dc, 2)], o_recv.at[0, c], device(3 - x, z, y, lax.rem(c + dc, 2))) for dc in (0, 1)
+    ]
+    o_send[1, 1 - c] = acc_o[1 - c, :, 0:128].astype(BF16)
+    last.append(wires(o_send.at[1, 1 - c], o_recv.at[1, c], sibling))
     for copy in last:
         copy.wait_recv()
-    for k in range(2):
-        total = o_recv[0, k].astype(F32)
-        for xx in (1, 2, 3):
-            total = total + o_recv[xx, k].astype(F32)
-        out[0, :, k * 128:(k + 1) * 128] = total.astype(BF16)
+    out[0, :, half_lanes(c)] = (acc_o[c, :, 0:128] + o_recv[0, c].astype(F32)).astype(BF16)
+    other = o_recv[1, 1 - c].astype(F32) + o_recv[0, 1 - c].astype(F32)
+    out[0, :, half_lanes(1 - c)] = other.astype(BF16)
 
     for copy in wires.all:
         copy.wait_send()
@@ -450,20 +566,19 @@
             pltpu.VMEM((4, 144, 256), BF16),
             pltpu.VMEM((4, 8, 256), F32),
             pltpu.VMEM((8, 8, 256), F32),
-            pltpu.VMEM((576, 256), F32),
-            pltpu.VMEM((4, 2, 144, 128), BF16),
+            pltpu.VMEM((4, 8, 256), F32),
+            pltpu.VMEM((288, 128), F32),
             pltpu.VMEM((2, 4, 2, 2, 4, 144, 128), BF16),
             pltpu.VMEM((4608, 256), BF16),
             pltpu.VMEM((544, 4608), BF16),
-            pltpu.VMEM((2, 576, 2048), BF16),
+            pltpu.VMEM((2, 576, 4096), BF16),
             pltpu.VMEM((2, 544, 256), F32),
             pltpu.VMEM((4, 512, 128), BF16),
             pltpu.VMEM((4, 512, 128), BF16),
             pltpu.VMEM((4, 32, 128), F32),
             pltpu.VMEM((4, 32, 128), F32),
             pltpu.VMEM((2, 512, 128), BF16),
-            pltpu.VMEM((2048, 256), BF16),
-            pltpu.VMEM((2048, 256), BF16),
+            pltpu.VMEM((2048, 512), BF16),
             pltpu.VMEM((256, 2048), BF16),
             pltpu.VMEM((128, 256), F32),
             pltpu.VMEM((128, 256), F32),
@@ -471,14 +586,16 @@
             pltpu.VMEM((2304, 256), BF16),
             pltpu.VMEM((256, 256), BF16),
             pltpu.VMEM((2, 256, 128), BF16),
-            pltpu.VMEM((4, 2, 64, 128), BF16),
-            pltpu.VMEM((2, 4, 2, 2, 4, 64, 128), BF16),
+            pltpu.VMEM((4, 4, 2, 256, 128), BF16),
             pltpu.VMEM((2, 576, 256), F32),
-            pltpu.VMEM((4, 2, 576, 128), BF16),
-            pltpu.VMEM((4, 2, 576, 128), BF16),
-            pltpu.SemaphoreType.DMA((200,)),
-            pltpu.SemaphoreType.DMA((200,)),
+            pltpu.VMEM((2, 2, 576, 128), BF16),
+            pltpu.VMEM((2, 2, 576, 128), BF16),
+            pltpu.SemaphoreType.DMA((240,)),
+            pltpu.SemaphoreType.DMA((240,)),
             pltpu.SemaphoreType.DMA((16,)),
+            pltpu.SemaphoreType.DMA((8,)),
+            pltpu.SemaphoreType.DMA((8,)),
+            pltpu.SemaphoreType.DMA((2,)),
         ],
         compiler_params=pltpu.CompilerParams(
             collective_id=0, has_side_effects=True, vmem_limit_bytes=56 * 1024 * 1024

time: 120 us -> 110 us (0.917)
  Pallas kernels: 117 us -> 108 us
    pallas_call x1, Pallas kernels: 117 us -> 108 us  [body(): pl.pallas_call(kernel, out_shape=jax.ShapeDtypeStruct((1, 576, 256), BF16...]
where the time goes in v3:
time: 110 us
  Pallas kernels  108 us (98%)
  local copies, waits for them, and re-layouts  1.69 us (2%)
    pallas_call x1, Pallas kernels, body(): pl.pallas_call(kernel, out_shape=jax.ShapeDtypeStruct((1, 576, 256), BF16...  108 us

profile of v3, /device:TPU:1, one launch (start us, length us, event | category | flops | bytes accessed | tf_op | source)
XLA Modules:
  0.0 110.1 jit_solution(16470419929196301418)
XLA Ops:
  0.7 107.7 %shard_map.73 = bf16[1,576,256]{2,1,0:T(8,128)(2,1)} custom-call(bf16[1,576,256]{2,1,0:T(8,128)(2,1)} %bitcast.7, f32[144,128]{1,0:T(8,128)} %bitcast.9, bf16[4608,256]{1,0:T(8,128)(2,1)} %w_query.1, bf16[16,4608]{1,0:T(8,128)(2,1)} %bitcast.8, bf16[576,2048]{1,0:T(8,128)(2,1)} %bitcast.5, bf16[1,64,512]{2,1,0:T(8,128)(2,1)} %cache.1, s32[1]{0:T(128)S(6)} %copy.9.lengths), custom_call_target="tpu_custom_call" | custom-call | tf_op jit(solution)/shard_map/pallas_call | solution.py:559
  108.4 1.7 %copy.10 = bf16[1,256,576]{1,2,0:T(8,128)(2,1)} copy(bf16[1,256,576]{1,2,0:T(8,128)(2,1)} %bitcast.6) | data formatting | bytes 589824

commit v4 on v3

--- a/solution.py
+++ b/solution.py
@@ -12,22 +12,37 @@
 F32 = jnp.float32
 BF16 = jnp.bfloat16
 LEFT = (((0,), (0,)), ((), ()))
+POOL = 72
+RECV = 77
 
 
 class Wires:
-    def __init__(self, send, recv):
-        self.send, self.recv, self.used, self.all = send, recv, 0, []
+    def __init__(self, send, recv, pool):
+        self.send, self.recv, self.pool, self.used, self.all = send, recv, pool, 0, []
 
     def __call__(self, src, dst, target):
-        k = self.used
         self.used += 1
+        return self.start(src, dst, target, self.recv.at[self.used - 1])
+
+    def branch(self, recv):
+        slots = iter(range(64))
+        return lambda src, dst, target: self.start(src, dst, target, recv.at[next(slots)])
+
+    def start(self, src, dst, target, recv):
+        n = len(self.all)
+        if n >= self.pool:
+            self.all[n - self.pool].wait_send()
         copy = pltpu.make_async_remote_copy(
-            src_ref=src, dst_ref=dst, send_sem=self.send.at[k], recv_sem=self.recv.at[k],
+            src_ref=src, dst_ref=dst, send_sem=self.send.at[n % self.pool], recv_sem=recv,
             device_id=target, device_id_type=MESH,
         )
         copy.start()
         self.all.append(copy)
         return copy
+
+    def finish(self):
+        for copy in self.all[-self.pool:]:
+            copy.wait_send()
 
 
 def near(v, d):
@@ -104,14 +119,19 @@
         copy.wait_recv()
     spread_b(3)
     yield
-    on_b(0)
     for j in range(1, 4):
         pass_a(j)
         pass_b(j)
-        zfp[j - 1].wait_recv()
-        zfm[j - 1].wait_recv()
-        on_a(j - 1)
+        if j == 2:
+            on_b(0)
+            zfp[0].wait_recv()
+            zfm[0].wait_recv()
+            on_a(0)
         yield
+    for j in (1, 2):
+        zfp[j].wait_recv()
+        zfm[j].wait_recv()
+        on_a(j)
     on_b(1)
     on_b(2)
     for copy in (zfp[3], zfm[3]):
@@ -194,7 +214,7 @@
     tokens, gain, w_query, w_keyval, w_out, cache, lengths, out,
     mine, raw, stat_y, stat_z, stat_x, gain_col, whole, w_rows, w_t, wo, acc, q_send, q_recv, kv_send, kv_recv,
     kv_t, slots, values_t, cosine, sine, scores, weights, queries, heads, heads_all, acc_o, o_send, o_recv,
-    send_sem, recv_sem, local_sem, block_send, block_recv, swap_sem,
+    send_sem, recv_sem, gather_sem, local_sem, block_send, block_recv, swap_send, swap_recv,
 ):
     x = lax.axis_index("gx")
     yz = lax.axis_index("yz")
@@ -204,14 +224,14 @@
         return (xx, zz * 8 + yy * 2 + cc)
 
     peer_x = lambda d, dc=0: device(near(x, d), z, y, lax.rem(c + dc, 2))
-    peer_y = lambda d: device(x, z, near(y, d), c)
+    peer_y = lambda d, dc=0: device(x, z, near(y, d), lax.rem(c + dc, 2))
     peer_z = lambda d, dc=0: device(x, near(z, d), y, lax.rem(c + dc, 2))
     sibling = device(x, z, y, 1 - c)
 
     barrier = pltpu.get_barrier_semaphore()
     peers = [sibling]
     for d in (1, 2, 3):
-        peers += [peer_x(d), peer_x(d, 1), peer_z(d), peer_z(d, 1), peer_y(d)]
+        peers += [peer_x(d), peer_x(d, 1), peer_z(d), peer_z(d, 1), peer_y(d), peer_y(d, 1)]
     twin = device(3 - x, 3 - z, y, c)
     peers.append(twin)
     for p in peers:
@@ -238,14 +258,14 @@
     wo_lanes = pl.ds(pl.multiple_of((x % 2) * 2048, 128), 2048)
     wo_other = pl.ds(pl.multiple_of((1 - x % 2) * 2048, 128), 2048)
     own_wo = local(w_out, wo.at[c, :, wo_lanes])
-    wo_rows = lambda k: pl.ds(k * 48, 48)
+    wo_rows = lambda k: pl.ds((0, 96, 432)[k], (96, 336, 144)[k])
 
     def lend(k):
         return wires(w_out.at[wo_rows(k), :], wo.at[c, wo_rows(k), wo_lanes], partner)
 
 
     pl.semaphore_wait(barrier, len(peers))
-    wires = Wires(send_sem, recv_sem)
+    wires = Wires(send_sem, recv_sem, POOL)
     first = [wires(tokens.at[0, quarter(near(z, d)), :], raw.at[z], peer_z(d)) for d in (1, 3, 2)]
 
     spot = whole.at[x // 2, y, x % 2, c, z]
@@ -271,7 +291,7 @@
 
     own_raw.wait()
     start_block(0)
-    lent = [lend(k) for k in range(0)]
+    lent = [lend(0)]
 
     own_mine.wait()
     v = mine[...].astype(F32)
@@ -307,6 +327,12 @@
         col = jnp.sum(jnp.where(lane == sub + (g % 8) * 16, line, 0.0), axis=1, keepdims=True)
         gain_col[k * 16:(k + 1) * 16, :] = jnp.broadcast_to(col, (16, 128))
 
+    freq = jnp.exp(
+        lax.broadcasted_iota(jnp.int32, (128, 256), 0).astype(F32) * (-2.0 * math.log(10000.0) / HEAD)
+    )
+    angle = (lengths[0] + lax.broadcasted_iota(jnp.int32, (128, 256), 1)).astype(F32) * freq
+    cosine[...] = jnp.cos(angle)
+    sine[...] = jnp.sin(angle)
     for copy in stat_1:
         copy.wait_recv()
     mean, square = join(stat_y, 4, 576.0)
@@ -331,6 +357,14 @@
     start_block(2)
     next(cached)
     next(cached)
+    own_rows.wait()
+    w_mine = pl.ds(pl.multiple_of(c * 256, 256), 256)
+
+    @pl.loop(0, 18)
+    def _(s):
+        at = pl.ds(pl.multiple_of(s * 256, 256), 256)
+        w_t[w_mine, at] = w_rows[at, :].T
+
     for k in range(8):
         pltpu.make_async_copy(raw.at[0, :, 0:128], whole.at[k // 4, y, (k // 2) % 2, k % 2, z], block_recv.at[k]).wait()
     for copy in stat_3:
@@ -364,19 +398,11 @@
             acc[half] += part
 
     yj = [y, near(y, -1), near(y, 1), near(y, 2)]
-    lent += [lend(k) for k in range(0, 7)]
-    gathered = gather_plane(wires, unit, peer_y, peer_z, y, z, lambda j: project(0, yj[j], j == 0), lambda j: project(1, yj[j], j == 0))
+    lent.append(lend(1))
+    gathered = gather_plane(wires.branch(gather_sem), unit, peer_y, peer_z, y, z, lambda j: project(0, yj[j], j == 0), lambda j: project(1, yj[j], j == 0), True)
     next(gathered)
     next(gathered)
     next(gathered)
-    own_rows.wait()
-    w_mine = pl.ds(pl.multiple_of(c * 256, 256), 256)
-
-    @pl.loop(0, 18)
-    def _(s):
-        at = pl.ds(pl.multiple_of(s * 256, 256), 256)
-        w_t[w_mine, at] = w_rows[at, :].T
-
     own_kv.wait()
     own_wo.wait()
     shared = [
@@ -394,38 +420,35 @@
         pass
     share = slots.reshape(16, 2, 64, 512).at[:, c]
     share_slots = wires(share, share, sibling)
-    freq = jnp.exp(
-        lax.broadcasted_iota(jnp.int32, (128, 256), 0).astype(F32) * (-2.0 * math.log(10000.0) / HEAD)
-    )
-    angle = (lengths[0] + lax.broadcasted_iota(jnp.int32, (128, 256), 1)).astype(F32) * freq
-    cosine[...] = jnp.cos(angle)
-    sine[...] = jnp.sin(angle)
     for _ in gathered:
         pass
+    third, fourth = [], []
+    lanes = lambda b: slice((b % 2) * 128, (b % 2) * 128 + 128)
     for b in range(4):
-        lanes = slice((b % 2) * 128, (b % 2) * 128 + 128)
-        kv_send[b] = acc[b // 2, 512:544, lanes]
-        q_send[b] = acc[b // 2, 0:512, lanes].astype(BF16)
-    third, fourth = [], []
+        kv_send[b] = acc[b // 2, 512:544, lanes(b)]
     for d in (1, 3, 2):
         third.append(wires(kv_send.at[near(x, d)], kv_recv.at[x], peer_x(d)))
-    for d in (1, 3, 2):
-        fourth.append(wires(q_send.at[near(x, d)], q_recv.at[x], peer_x(d)))
+    for h in range(2):
+        for b in range(4):
+            q_send[b, h] = acc[b // 2, h * 256:(h + 1) * 256, lanes(b)].astype(BF16)
+        fourth.append([wires(q_send.at[near(x, d), h], q_recv.at[x, h], peer_x(d)) for d in (1, 3, 2)])
     for copy in third:
         copy.wait_recv()
     total = kv_send[x]
     for d in (1, 2, 3):
         total = total + kv_recv[near(x, d)]
-    kv_block = lambda zz, yy: kv_t.at[c, pl.ds(pl.multiple_of((zz * 4 + yy) * 32, 32), 32), :]
-    kv_t[c, pl.ds(pl.multiple_of((z * 4 + y) * 32, 32), 32), :] = total.astype(BF16)
-    kv_y = [wires(kv_block(z, y), kv_block(z, y), peer_y(d)) for d in (1, 3, 2)]
+    for k in range(2):
+        kv_t[c, z, y, k] = total[k * 16:(k + 1) * 16].astype(BF16)
+    kv_y = [wires(kv_t.at[c, z, y, 0], kv_t.at[c, z, y, 0], peer_y(d)) for d in (1, 3, 2)]
+    kv_z = [wires(kv_t.at[c, z, y, 1], kv_t.at[c, z, y, 1], peer_z(d)) for d in (1, 3, 2)]
+    line_y, line_z = kv_t.at[c, z, :, 0], kv_t.at[c, :, y, 1]
     for copy in kv_y:
         copy.wait_recv()
-    kv_rows = kv_t.at[c, pl.ds(pl.multiple_of(z * 128, 128), 128), :]
-    kv_z = [wires(kv_rows, kv_rows, sibling)]
-    for d in (1, 3, 2):
-        for dc in (0, 1):
-            kv_z.append(wires(kv_rows, kv_rows, peer_z(d, dc)))
+    kv_last = [wires(line_y, line_y, peer_z(d, dc)) for dc in (0, 1) for d in (1, 3, 2)]
+    for copy in kv_z:
+        copy.wait_recv()
+    kv_last += [wires(line_z, line_z, peer_y(d, dc)) for dc in (0, 1) for d in (1, 3, 2)]
+    kv_last += [wires(line_y, line_y, sibling), wires(line_z, line_z, sibling)]
     share_slots.wait_recv()
 
     @pl.loop(0, 8)
@@ -434,105 +457,111 @@
         values_t[:, at] = slots[at, 256:512].T
 
 
-    for copy in fourth:
-        copy.wait_recv()
-    lent += [lend(k) for k in range(7, 12)]
-    query = q_send[x].astype(F32)
-    for d in (1, 2, 3):
-        query = query + q_recv[near(x, d)].astype(F32)
+    inv = 1.0 / math.sqrt(HEAD)
     cos_q, sin_q = cosine[:, half_lanes(c)], sine[:, half_lanes(c)]
+    passed = []
+
+    def pass_weights(chunks):
+        for k in chunks:
+            lent[k].wait_recv()
+            passed.append(wires(wo.at[c, wo_rows(k), wo_other], wo.at[c, wo_rows(k), wo_other], sibling))
+
+    def fold(s, f):
+        return f(s.reshape(s.shape[0] // 8, 8, 128), axis=0)
+
+    def rotated(u, w, cos, sin):
+        return jnp.concatenate([u * cos - w * sin, w * cos + u * sin], axis=0).astype(BF16)
+
+    stays = z // 2 == pair
+
+    def swap(h):
+        return pltpu.make_async_remote_copy(
+            src_ref=heads.at[h], dst_ref=heads_all.at[y, 3 - z, h], send_sem=swap_send.at[h], recv_sem=swap_recv.at[h],
+            device_id=twin, device_id_type=MESH,
+        )
+
+    def keep(h):
+        return pltpu.make_async_copy(heads.at[h], heads_all.at[y, z, h], swap_recv.at[h])
+
     for h in range(2):
-        u, w = query[h * 256:h * 256 + 128], query[h * 256 + 128:h * 256 + 256]
-        queries[0:128, h * 128:(h + 1) * 128] = (u * cos_q - w * sin_q).astype(BF16)
-        queries[128:256, h * 128:(h + 1) * 128] = (w * cos_q + u * sin_q).astype(BF16)
-    inv = 1.0 / math.sqrt(HEAD)
-
-    def fold(s, f):
-        return f(s.reshape(s.shape[0] // 8, 8, 256), axis=0)
-
-    def cached_scores(k, top):
-        at = pl.ds(pl.multiple_of(k * 256, 256), 256)
-        s = jnp.dot(slots[at, 0:256], queries[...], preferred_element_type=F32) * inv
-        slot = k * 256 + lax.broadcasted_iota(jnp.int32, (256, 256), 0)
-        s = jnp.where(slot < lengths[0], s, -1e30)
-        scores[at, :] = s
-        return jnp.maximum(top, fold(s, jnp.max))
-
-    top = lax.fori_loop(0, 8, cached_scores, jnp.full((8, 256), -1e30, F32))
-    for copy in kv_z:
-        copy.wait_recv()
-    kv = jnp.concatenate([kv_t[0], kv_t[1]], axis=1)
-    u, w = kv[0:128].astype(F32), kv[128:256].astype(F32)
-    fresh = jnp.concatenate([u * cosine[...] - w * sine[...], w * cosine[...] + u * sine[...]], axis=0).astype(BF16)
-    s = lax.dot_general(fresh, queries[...], LEFT, preferred_element_type=F32) * inv
-    t = c * 128 + lax.rem(lax.broadcasted_iota(jnp.int32, (256, 256), 1), 128)
-    t2 = lax.broadcasted_iota(jnp.int32, (256, 256), 0)
-    s = jnp.where(t2 <= t, s, -1e30)
-    scores[2048:2304, :] = s
-    top = jnp.max(jnp.maximum(top, fold(s, jnp.max)), axis=0, keepdims=True)
-
-    def exponentials(k, total):
-        at = pl.ds(pl.multiple_of(k * 256, 256), 256)
-        p = jnp.exp(scores[at, :] - top)
-        weights[at, :] = p.astype(BF16)
-        return total + fold(p, jnp.sum)
-
-    total = jnp.sum(lax.fori_loop(0, 9, exponentials, jnp.zeros((8, 256), F32)), axis=0, keepdims=True)
-    summed = jnp.dot(values_t[...], weights[0:2048, :], preferred_element_type=F32)
-    summed += jnp.dot(kv[256:512], weights[2048:2304, :], preferred_element_type=F32)
-    done = (summed / total).astype(BF16)
-    heads[0] = done[:, 0:128]
-    heads[1] = done[:, 128:256]
-
-    stays = z // 2 == pair
-    swap = pltpu.make_async_remote_copy(
-        src_ref=heads, dst_ref=heads_all.at[y, 3 - z], send_sem=swap_sem.at[0], recv_sem=swap_sem.at[1],
-        device_id=twin, device_id_type=MESH,
-    )
-    keep = pltpu.make_async_copy(heads, heads_all.at[y, z], swap_sem.at[1])
-    pl.when(stays)(keep.start)
-    pl.when(jnp.logical_not(stays))(swap.start)
-    passed = []
-    for k in range(7):
-        lent[k].wait_recv()
-        passed.append(wires(wo.at[c, wo_rows(k), wo_other], wo.at[c, wo_rows(k), wo_other], sibling))
-    shared[2].wait_recv()
-    keep.wait()
-    pl.when(jnp.logical_not(stays))(swap.wait_send)
-
-    def head_unit(zz, yy, start, count):
-        return heads_all.at[yy, zz, start // 2, (start % 2) * 128:(start % 2 + count) * 128, :]
-
-    def project_out(h, yy, fresh_start):
+        for copy in fourth[h]:
+            copy.wait_recv()
+        if h:
+            lent.append(lend(2))
+        query = q_send[x, h].astype(F32)
+        for d in (1, 2, 3):
+            query = query + q_recv[near(x, d), h].astype(F32)
+        queries[...] = rotated(query[0:128], query[128:256], cos_q, sin_q)
+
+        def cached_scores(k, top):
+            at = pl.ds(pl.multiple_of(k * 256, 256), 256)
+            s = jnp.dot(slots[at, 0:256], queries[...], preferred_element_type=F32) * inv
+            slot = k * 256 + lax.broadcasted_iota(jnp.int32, (256, 128), 0)
+            s = jnp.where(slot < lengths[0], s, -1e30)
+            scores[at, :] = s
+            return jnp.maximum(top, fold(s, jnp.max))
+
+        top = lax.fori_loop(0, 8, cached_scores, jnp.full((8, 128), -1e30, F32))
+        if h == 0:
+            for copy in kv_last:
+                copy.wait_recv()
+            kv = jnp.concatenate([kv_t[k].reshape(512, 128) for k in range(2)], axis=1)
+            fresh = rotated(kv[0:128].astype(F32), kv[128:256].astype(F32), cosine[...], sine[...])
+        s = lax.dot_general(fresh, queries[...], LEFT, preferred_element_type=F32) * inv
+        t = c * 128 + lax.broadcasted_iota(jnp.int32, (256, 128), 1)
+        t2 = lax.broadcasted_iota(jnp.int32, (256, 128), 0)
+        s = jnp.where(t2 <= t, s, -1e30)
+        scores[2048:2304, :] = s
+        top = jnp.max(jnp.maximum(top, fold(s, jnp.max)), axis=0, keepdims=True)
+
+        def exponentials(k, total):
+            at = pl.ds(pl.multiple_of(k * 256, 256), 256)
+            p = jnp.exp(scores[at, :] - top)
+            weights[at, :] = p.astype(BF16)
+            return total + fold(p, jnp.sum)
+
+        total = jnp.sum(lax.fori_loop(0, 9, exponentials, jnp.zeros((8, 128), F32)), axis=0, keepdims=True)
+        summed = jnp.dot(values_t[...], weights[0:2048, :], preferred_element_type=F32)
+        summed += jnp.dot(kv[256:512], weights[2048:2304, :], preferred_element_type=F32)
+        heads[h] = (summed / total).astype(BF16)
+        pl.when(stays)(keep(h).start)
+        pl.when(jnp.logical_not(stays))(swap(h).start)
+
+    begun = []
+
+    def project_out(h, j):
+        if not begun:
+            for copy in passed:
+                copy.wait_recv()
         rights, lanes = [], []
-        for j in range(2):
-            block = 2 * pair + j
-            rights.append(jnp.concatenate([heads_all[yy, block, h], heads_all[yy, 3 - block, h]], axis=1))
-            lanes.append(pl.ds(pl.multiple_of(j * 2048 + yy * 512 + h * 256, 128), 256))
+        for k in range(2):
+            block = 2 * pair + k
+            rights.append(jnp.concatenate([heads_all[yj[j], block, h], heads_all[yj[j], 3 - block, h]], axis=1))
+            lanes.append(pl.ds(pl.multiple_of(k * 2048 + yj[j] * 512 + h * 256, 128), 256))
         right = jnp.concatenate(rights, axis=0)
         for k in range(2):
             left = jnp.concatenate([wo[k, :, lanes[0]], wo[k, :, lanes[1]]], axis=1)
             part = jnp.dot(left, right, preferred_element_type=F32)
-            if fresh_start:
+            if begun:
+                acc_o[k] += part
+            else:
                 acc_o[k] = part
-            else:
-                acc_o[k] += part
-
-    begun = []
-
-    def absorb(h, j):
-        if not begun:
-            for copy in passed:
-                copy.wait_recv()
-        project_out(h, yj[j], not begun)
         begun.append(j)
 
-    heads_gather = gather_plane(wires, head_unit, peer_y, peer_z, y, z, lambda j: absorb(0, j), lambda j: absorb(1, j), direct=True)
-    for step in range(4):
+    head_unit = lambda zz, yy, start, count: heads_all.at[yy, zz, start // 2, (start % 2) * 128:(start % 2 + count) * 128, :]
+    pass_weights((0, 1))
+    for h in range(2):
+        keep(h).wait()
+    heads_gather = gather_plane(
+        wires.branch(gather_sem), head_unit, peer_y, peer_z, y, z, lambda j: project_out(0, j), lambda j: project_out(1, j), direct=True
+    )
+    next(heads_gather)
+    for h in range(2):
+        pl.when(jnp.logical_not(stays))(swap(h).wait_send)
+    for step in range(3):
         next(heads_gather)
-    for k in range(7, 12):
-        lent[k].wait_recv()
-        passed.append(wires(wo.at[c, wo_rows(k), wo_other], wo.at[c, wo_rows(k), wo_other], sibling))
+    shared[2].wait_recv()
+    pass_weights((2,))
     for _ in heads_gather:
         pass
     for k in range(2):
@@ -548,8 +577,8 @@
     other = o_recv[1, 1 - c].astype(F32) + o_recv[0, 1 - c].astype(F32)
     out[0, :, half_lanes(1 - c)] = other.astype(BF16)
 
-    for copy in wires.all:
-        copy.wait_send()
+    wires.finish()
+    assert wires.used <= RECV and len(locals_) <= 8
 
 
 def body(tokens, gain, w_query, w_keyval, w_out, cache, lengths):
@@ -573,28 +602,30 @@
             pltpu.VMEM((544, 4608), BF16),
             pltpu.VMEM((2, 576, 4096), BF16),
             pltpu.VMEM((2, 544, 256), F32),
-            pltpu.VMEM((4, 512, 128), BF16),
-            pltpu.VMEM((4, 512, 128), BF16),
+            pltpu.VMEM((4, 2, 256, 128), BF16),
+            pltpu.VMEM((4, 2, 256, 128), BF16),
             pltpu.VMEM((4, 32, 128), F32),
             pltpu.VMEM((4, 32, 128), F32),
-            pltpu.VMEM((2, 512, 128), BF16),
+            pltpu.VMEM((2, 4, 4, 2, 16, 128), BF16),
             pltpu.VMEM((2048, 512), BF16),
             pltpu.VMEM((256, 2048), BF16),
             pltpu.VMEM((128, 256), F32),
             pltpu.VMEM((128, 256), F32),
-            pltpu.VMEM((2304, 256), F32),
-            pltpu.VMEM((2304, 256), BF16),
-            pltpu.VMEM((256, 256), BF16),
+            pltpu.VMEM((2304, 128), F32),
+            pltpu.VMEM((2304, 128), BF16),
+            pltpu.VMEM((256, 128), BF16),
             pltpu.VMEM((2, 256, 128), BF16),
             pltpu.VMEM((4, 4, 2, 256, 128), BF16),
             pltpu.VMEM((2, 576, 256), F32),
             pltpu.VMEM((2, 2, 576, 128), BF16),
             pltpu.VMEM((2, 2, 576, 128), BF16),
-            pltpu.SemaphoreType.DMA((240,)),
-            pltpu.SemaphoreType.DMA((240,)),
-            pltpu.SemaphoreType.DMA((16,)),
+            pltpu.SemaphoreType.DMA((POOL,)),
+            pltpu.SemaphoreType.DMA((RECV,)),
+            pltpu.SemaphoreType.DMA((40,)),
             pltpu.SemaphoreType.DMA((8,)),
             pltpu.SemaphoreType.DMA((8,)),
+            pltpu.SemaphoreType.DMA((8,)),
+            pltpu.SemaphoreType.DMA((2,)),
             pltpu.SemaphoreType.DMA((2,)),
         ],
         compiler_params=pltpu.CompilerParams(

time: 110 us -> 102 us (0.927)
  Pallas kernels: 108 us -> 99.5 us
    pallas_call x1, Pallas kernels: 108 us -> 99.5 us  [body(): pl.pallas_call(kernel, out_shape=jax.ShapeDtypeStruct((1, 576, 256), BF16...]
where the time goes in v4:
time: 102 us
  Pallas kernels  99.5 us (98%)
  local copies, waits for them, and re-layouts  1.69 us (2%)
    pallas_call x1, Pallas kernels, body(): pl.pallas_call(kernel, out_shape=jax.ShapeDtypeStruct((1, 576, 256), BF16...  99.5 us

profile of v4, /device:TPU:1, one launch (start us, length us, event | category | flops | bytes accessed | tf_op | source)
XLA Modules:
  0.0 101.8 jit_solution(15371574247836013120)
XLA Ops:
  0.7 99.5 %shard_map.73 = bf16[1,576,256]{2,1,0:T(8,128)(2,1)} custom-call(bf16[1,576,256]{2,1,0:T(8,128)(2,1)} %bitcast.7, f32[144,128]{1,0:T(8,128)} %bitcast.9, bf16[4608,256]{1,0:T(8,128)(2,1)} %w_query.1, bf16[16,4608]{1,0:T(8,128)(2,1)} %bitcast.8, bf16[576,2048]{1,0:T(8,128)(2,1)} %bitcast.5, bf16[1,64,512]{2,1,0:T(8,128)(2,1)} %cache.1, s32[1]{0:T(128)S(6)} %copy.9.lengths), custom_call_target="tpu_custom_call" | custom-call | tf_op jit(solution)/shard_map/pallas_call | solution.py:588
  100.1 1.7 %copy.10 = bf16[1,256,576]{1,2,0:T(8,128)(2,1)} copy(bf16[1,256,576]{1,2,0:T(8,128)(2,1)} %bitcast.6) | data formatting | bytes 589824

commit v5 on v4

--- a/solution.py
+++ b/solution.py
@@ -486,7 +486,7 @@
     for h in range(2):
         for copy in fourth[h]:
             copy.wait_recv()
-        if h:
+        if not h:
             lent.append(lend(2))
         query = q_send[x, h].astype(F32)
         for d in (1, 2, 3):
@@ -558,17 +558,17 @@
     next(heads_gather)
     for h in range(2):
         pl.when(jnp.logical_not(stays))(swap(h).wait_send)
-    for step in range(3):
+    for step in range(2):
         next(heads_gather)
     shared[2].wait_recv()
     pass_weights((2,))
     for _ in heads_gather:
         pass
-    for k in range(2):
-        o_send[0, k] = acc_o[k, :, 128:256].astype(BF16)
-    last = [
-        wires(o_send.at[0, lax.rem(c + dc, 2)], o_recv.at[0, c], device(3 - x, z, y, lax.rem(c + dc, 2))) for dc in (0, 1)
-    ]
+    last = []
+    for dc in (0, 1):
+        cc = lax.rem(c + dc, 2)
+        o_send[0, cc] = acc_o[cc, :, 128:256].astype(BF16)
+        last.append(wires(o_send.at[0, cc], o_recv.at[0, c], device(3 - x, z, y, cc)))
     o_send[1, 1 - c] = acc_o[1 - c, :, 0:128].astype(BF16)
     last.append(wires(o_send.at[1, 1 - c], o_recv.at[1, c], sibling))
     for copy in last:

time: 102 us -> 102 us (level)
  no operation moved by 1% of the time
where the time goes in v5:
time: 102 us
  Pallas kernels  99.3 us (97%)
  local copies, waits for them, and re-layouts  1.69 us (2%)
    pallas_call x1, Pallas kernels, body(): pl.pallas_call(kernel, out_shape=jax.ShapeDtypeStruct((1, 576, 256), BF16...  99.3 us

profile of v5, /device:TPU:1, one launch (start us, length us, event | category | flops | bytes accessed | tf_op | source)
XLA Modules:
  0.0 101.7 jit_solution(10230701750955510866)
XLA Ops:
  0.7 99.3 %shard_map.73 = bf16[1,576,256]{2,1,0:T(8,128)(2,1)} custom-call(bf16[1,576,256]{2,1,0:T(8,128)(2,1)} %bitcast.7, f32[144,128]{1,0:T(8,128)} %bitcast.9, bf16[4608,256]{1,0:T(8,128)(2,1)} %w_query.1, bf16[16,4608]{1,0:T(8,128)(2,1)} %bitcast.8, bf16[576,2048]{1,0:T(8,128)(2,1)} %bitcast.5, bf16[1,64,512]{2,1,0:T(8,128)(2,1)} %cache.1, s32[1]{0:T(128)S(6)} %copy.9.lengths), custom_call_target="tpu_custom_call" | custom-call | tf_op jit(solution)/shard_map/pallas_call | solution.py:588
  100.0 1.7 %copy.10 = bf16[1,256,576]{1,2,0:T(8,128)(2,1)} copy(bf16[1,256,576]{1,2,0:T(8,128)(2,1)} %bitcast.6) | data formatting | bytes 589824
